TPU v7x, 512 devices: a whole 4x4x16 slice. The times are simulated.
512 devices in a mesh: seq: 16 (over z), section: 8 (over x, core), dp: 4 (over y).
Axes of the slice: x: 4, y: 4, z: 16, core: 2. Of those that a mesh axis runs over, the one named last changes fastest.
Arguments:
- queries: bfloat16 [8, 4, 2048, 4096], P('section', 'dp', 'seq'), may hold values from -160 to 160
- keys: bfloat16 [8, 4, 2048, 512], P('section', 'dp', 'seq'), may hold values from -6 to 6
- output_gradient: bfloat16 [8, 4, 2048, 4096], P('section', 'dp', 'seq'), may hold values from -6 to 6
- rollout_index: int32 [8, 4, 2048], P('section', 'dp'), may hold values from 0 to 15, never falling along the last dimension, each value on 1 to 384 neighbouring positions
- loss_token_mask: int32 [8, 4, 2048], P('section', 'dp'), may hold values 0 or 1
- advantages: float32 [8, 4, 16], P('section', 'dp'), may hold values from -4 to 4
- value_projection: bfloat16 [8, 8192, 512], P('section', ('seq', 'dp')), may hold values from -0.25 to 0.25
- adapter_down_weight: bfloat16 [8, 8192, 64], P('section', ('seq', 'dp')), may hold values from -0.75 to 0.75
- adapter_up_weight: bfloat16 [8, 64, 512], P('section'), may hold values from -0.25 to 0.25
- adapter_activation: bfloat16 [8, 4, 2048, 64], P('section', 'dp', 'seq'), may hold values from -6 to 6
Outputs:
- handed: bfloat16 [8, 4, 2048, 8192], P('section', 'dp', 'seq')
- adapter_up_gradient: float32 [8, 64, 512], P('section', ('seq', 'dp'))
Inputs may be any that keep to these rules, and one draw needn't show every extreme that they name: `rollout_index`: each rollout's tokens form one run; at most 384 tokens a rollout.
All inputs are finite; a program needn't handle non-finite values. No bound on the sum of `loss_token_mask` on one device may be relied on, other than what follows from the above.
Results may differ from a plain program's by a relative error of at most 0.015.
Values may be sent and summed in bfloat16 or wider, within the bound.
No kernel may reach another device: no remote copies, remote signals or barrier semaphores. Data moves between devices by JAX's collectives and lax.ppermute only.
A program may use at most 128 MiB of HBM per device.

v0:
```python
import jax
import jax.numpy as jnp
from jax import lax
from jax.sharding import PartitionSpec as P

HEAD_SIZE = 128


NEG_FILL = -1e30


def passed_along(value, axis, steps):
    count = lax.axis_size(axis)
    first, last = (max(0, -steps), min(count, count - steps))
    return lax.ppermute(value, axis, [(source, source + steps) for source in range(first, last)])


def token_weights(rollout_row, token_mask_row, advantage_values):
    onehot = (
        rollout_row[:, None] == jnp.arange(advantage_values.shape[0], dtype=jnp.int32)[None, :]
    ).astype(jnp.float32)
    return jnp.sum(onehot * advantage_values[None, :], axis=1) * token_mask_row.astype(jnp.float32)


def local(
    queries,
    keys,
    output_gradient,
    rollout_index,
    loss_token_mask,
    advantages,
    value_projection,
    adapter_down_weight,
    adapter_up_weight,
    adapter_activation,
):
    seq_count = lax.axis_size("seq")
    local_rows = queries.shape[2]
    seq_len = local_rows * seq_count
    query_heads = queries.shape[3] // HEAD_SIZE
    heads_local = query_heads // seq_count
    kv_width = keys.shape[3]
    kv_heads = kv_width // HEAD_SIZE
    query_group_size = query_heads // kv_heads
    copies = query_group_size // heads_local
    gathered_q, gathered_g = (
        lax.all_to_all(queries[0, 0], "seq", split_axis=1, concat_axis=0, tiled=True),
        lax.all_to_all(output_gradient[0, 0], "seq", split_axis=1, concat_axis=0, tiled=True),
    )
    own_head = lax.axis_index("seq") * heads_local // query_group_size
    all_keys = lax.all_gather(keys[0, 0], "seq", axis=0, tiled=True)
    key_cols = lax.dynamic_slice_in_dim(all_keys, own_head * HEAD_SIZE, HEAD_SIZE, 1)
    rollout_row = rollout_index[0, 0]
    weights = token_weights(rollout_row, loss_token_mask[0, 0], advantages[0, 0])
    scaled = (gathered_g.astype(jnp.float32) * weights[:, None]).astype(jnp.bfloat16)
    query_heads_all = gathered_q.reshape(seq_len, heads_local, HEAD_SIZE)
    grad_heads_all = scaled.reshape(seq_len, heads_local, HEAD_SIZE)
    block_rows = min(512, seq_len)
    positions = jnp.arange(seq_len, dtype=jnp.int32)

    def add_block(block_index, summed_total):
        row_start = block_index * block_rows
        query_block = lax.dynamic_slice_in_dim(query_heads_all, row_start, block_rows, 0)
        grad_block = lax.dynamic_slice_in_dim(grad_heads_all, row_start, block_rows, 0)
        row_pos = row_start + jnp.arange(block_rows, dtype=jnp.int32)
        row_segment = lax.dynamic_slice_in_dim(rollout_row, row_start, block_rows, 0)
        allowed = (positions[None, :] <= row_pos[:, None]) & (
            rollout_row[None, :] == row_segment[:, None]
        )
        scores = jnp.einsum(
            "qhd,kd->hqk", query_block, key_cols, preferred_element_type=jnp.float32
        ) * HEAD_SIZE ** (-0.5)
        scores = jnp.where(allowed[None], scores, NEG_FILL)
        row_max = jnp.max(scores, axis=2, keepdims=True)
        exp_terms = jnp.where(allowed[None], jnp.exp(scores - row_max), 0.0)
        prob_bf = (exp_terms / jnp.sum(exp_terms, axis=2, keepdims=True)).astype(jnp.bfloat16)
        return summed_total + jnp.einsum(
            "hqk,qhd->kd", prob_bf, grad_block, preferred_element_type=jnp.float32
        )

    value_part = lax.fori_loop(
        0, seq_len // block_rows, add_block, jnp.zeros((seq_len, HEAD_SIZE), jnp.float32)
    )
    returned = lax.all_to_all(
        value_part.astype(jnp.bfloat16), "seq", split_axis=0, concat_axis=1, tiled=True
    ).astype(value_part.dtype)
    value_gradient = jnp.sum(returned.reshape(local_rows, kv_heads, copies, HEAD_SIZE), axis=2)
    value_gradient = value_gradient.reshape(local_rows, kv_width).astype(jnp.bfloat16)
    adapter_middle = lax.dot_general(
        value_gradient,
        adapter_up_weight[0],
        (((1,), (1,)), ((), ())),
        preferred_element_type=jnp.float32,
    ).astype(jnp.bfloat16)
    joined = jnp.concatenate([value_gradient, adapter_middle], axis=1)
    weight_joined = jnp.concatenate([value_projection[0], adapter_down_weight[0]], axis=1)
    layer_gradient = lax.dot_general(
        joined,
        lax.all_gather(weight_joined, ("seq", "dp"), axis=0, tiled=True),
        (((1,), (1,)), ((), ())),
        preferred_element_type=jnp.float32,
    ).astype(jnp.bfloat16)
    handed = passed_along(layer_gradient, "section", -1)
    adapter_term = lax.dot_general(
        adapter_activation[0, 0],
        value_gradient,
        (((0,), (0,)), ((), ())),
        preferred_element_type=jnp.float32,
    )
    adapter_up_gradient = lax.psum_scatter(
        adapter_term, ("seq", "dp"), scatter_dimension=0, tiled=True
    )
    return (handed[None, None], adapter_up_gradient[None])


def solution(mesh):
    placed = (
        P("section", "dp", "seq", None),
        P("section", "dp", "seq", None),
        P("section", "dp", "seq", None),
        P("section", "dp", None),
        P("section", "dp", None),
        P("section", "dp", None),
        P("section", ("seq", "dp"), None),
        P("section", ("seq", "dp"), None),
        P("section", None, None),
        P("section", "dp", "seq", None),
    )
    return jax.shard_map(
        local,
        mesh=mesh,
        in_specs=placed,
        out_specs=(P("section", "dp", "seq", None), P("section", ("seq", "dp"), None)),
        check_vma=False,
    )
```

profile of v0, /device:TPU:4, one launch (start us, length us, event | category | flops | bytes accessed | tf_op | source)
XLA Modules:
  0.0 593.7 jit_solution(10740301622846501848)
XLA Ops:
  8.0 2.3 copy.41
  10.3 15.2 %all-to-all-start.1 = ((bf16[128,16,256]{0,2,1:T(8,128)(2,1)}), bf16[128,16,256]{0,2,1:T(8,128)(2,1)S(1)}, u32[]{:S(2)}, u32[]{:S(2)}) async-start(bf16[128,16,256]{0,2,1:T(8,128)(2,1)} %bitcast.4), calls=%async_computation.1 | async-start | bytes 2097152 | tf_op jit(solution)/shard_map/all_to_all | solution.py:48
  27.7 56.1 %all-to-all-done.1 = bf16[128,16,256]{0,2,1:T(8,128)(2,1)S(1)} async-done(((bf16[128,16,256]{0,2,1:T(8,128)(2,1)}), bf16[128,16,256]{0,2,1:T(8,128)(2,1)S(1)}, u32[]{:S(2)}, u32[]{:S(2)}) %all-to-all-start.1) | async-done | bytes 1048608 | tf_op jit(solution)/shard_map/all_to_all | solution.py:48
  83.8 9.2 %all-to-all-start = ((bf16[128,16,256]{0,2,1:T(8,128)(2,1)}), bf16[128,16,256]{0,2,1:T(8,128)(2,1)S(1)}, u32[]{:S(2)}, u32[]{:S(2)}) async-start(bf16[128,16,256]{0,2,1:T(8,128)(2,1)} %bitcast.1), calls=%async_computation | async-start | bytes 2097152 | tf_op jit(solution)/shard_map/all_to_all | solution.py:47
  93.4 2.5 copy.42
  96.0 1.7 reshape.126
  97.7 50.7 %all-to-all-done = bf16[128,16,256]{0,2,1:T(8,128)(2,1)S(1)} async-done(((bf16[128,16,256]{0,2,1:T(8,128)(2,1)}), bf16[128,16,256]{0,2,1:T(8,128)(2,1)S(1)}, u32[]{:S(2)}, u32[]{:S(2)}) %all-to-all-start) | async-done | bytes 1048608 | tf_op jit(solution)/shard_map/all_to_all | solution.py:47
  150.1 2.3 reshape.125
  152.4 1.9 dynamic-slice_bitcast_fusion
  154.4 64.1 %while.14 = (s32[]{:T(128)}, f32[2048,128]{1,0:T(8,128)}, s32[1,1,2048]{2,1,0:T(1,128)S(1)}, s32[2048]{0:T(1024)S(1)}, bf16[2048,2,128]{0,2,1:T(8,128)(2,1)}, /*...) while((s32[]{:T(128)}, f32[2048,128]{1,0:T(8,128)}, ...), condition=%wide.region_4.5_spmd.clone, body=%wide.region_1.4_spmd.clone.sunk | while | flops 1092094464 | bytes 23095476 | solution.py:81
  155.6 8.8 %fusion.64 = (f32[2,512]{1,0:T(2,128)S(1)}, f32[2,512,2048]{2,1,0:T(8,128)}) fusion(pred[512,2048]{1,0:T(8,128)(4,1)S(1)} %fusion.63, bf16[2048,128]{1,0:T(8,128)(2,1)} %get-tuple-element.286, bf16[2048,2,128]{0,2,1:T(8,128)(2,1)} %get-tuple-element.285, s32[]{:T(128)S(6)} %select_n.57), kind=kOutput, calls=%fused_computation.47.clone.1 | convolution fusion | flops 547358720 | bytes 11276292 | tf_op jit(solution)/shard_map/while/body/eval_jaxpr/sub | solution.py:75
  164.4 6.0 %fusion.65 = f32[2048,128]{1,0:T(8,128)} fusion(f32[2,512,2048]{2,1,0:T(8,128)} %get-tuple-element.257, f32[2,512]{1,0:T(2,128)S(1)} %get-tuple-element.258, f32[2048,128]{1,0:T(8,128)} %get-tuple-element.271, pred[]{:T(512)S(6)} %compare.5, bf16[2048,2,128]{0,2,1:T(8,128)(2,1)S(1)} %get-tuple-element.287, s32[]{:T(128)S(6)} %select_n.57), kind=kOutput, calls=%fused_computation.16.clone.1 | convolution fusion | flops 541589504 | bytes 10752005 | tf_op jit(solution)/shard_map/while/body/eval_jaxpr/hqk,qhd->kd/dot_general | solution.py:77
  171.4 8.8 %fusion.64 = (f32[2,512]{1,0:T(2,128)S(1)}, f32[2,512,2048]{2,1,0:T(8,128)}) fusion(pred[512,2048]{1,0:T(8,128)(4,1)S(1)} %fusion.63, bf16[2048,128]{1,0:T(8,128)(2,1)} %get-tuple-element.286, bf16[2048,2,128]{0,2,1:T(8,128)(2,1)} %get-tuple-element.285, s32[]{:T(128)S(6)} %select_n.57), kind=kOutput, calls=%fused_computation.47.clone.1 | convolution fusion | flops 547358720 | bytes 11276292 | tf_op jit(solution)/shard_map/while/body/eval_jaxpr/sub | solution.py:75
  180.2 6.2 %fusion.65 = f32[2048,128]{1,0:T(8,128)} fusion(f32[2,512,2048]{2,1,0:T(8,128)} %get-tuple-element.257, f32[2,512]{1,0:T(2,128)S(1)} %get-tuple-element.258, f32[2048,128]{1,0:T(8,128)} %get-tuple-element.271, pred[]{:T(512)S(6)} %compare.5, bf16[2048,2,128]{0,2,1:T(8,128)(2,1)S(1)} %get-tuple-element.287, s32[]{:T(128)S(6)} %select_n.57), kind=kOutput, calls=%fused_computation.16.clone.1 | convolution fusion | flops 541589504 | bytes 10752005 | tf_op jit(solution)/shard_map/while/body/eval_jaxpr/hqk,qhd->kd/dot_general | solution.py:77
  187.5 8.8 %fusion.64 = (f32[2,512]{1,0:T(2,128)S(1)}, f32[2,512,2048]{2,1,0:T(8,128)}) fusion(pred[512,2048]{1,0:T(8,128)(4,1)S(1)} %fusion.63, bf16[2048,128]{1,0:T(8,128)(2,1)} %get-tuple-element.286, bf16[2048,2,128]{0,2,1:T(8,128)(2,1)} %get-tuple-element.285, s32[]{:T(128)S(6)} %select_n.57), kind=kOutput, calls=%fused_computation.47.clone.1 | convolution fusion | flops 547358720 | bytes 11276292 | tf_op jit(solution)/shard_map/while/body/eval_jaxpr/sub | solution.py:75
  196.3 6.2 %fusion.65 = f32[2048,128]{1,0:T(8,128)} fusion(f32[2,512,2048]{2,1,0:T(8,128)} %get-tuple-element.257, f32[2,512]{1,0:T(2,128)S(1)} %get-tuple-element.258, f32[2048,128]{1,0:T(8,128)} %get-tuple-element.271, pred[]{:T(512)S(6)} %compare.5, bf16[2048,2,128]{0,2,1:T(8,128)(2,1)S(1)} %get-tuple-element.287, s32[]{:T(128)S(6)} %select_n.57), kind=kOutput, calls=%fused_computation.16.clone.1 | convolution fusion | flops 541589504 | bytes 10752005 | tf_op jit(solution)/shard_map/while/body/eval_jaxpr/hqk,qhd->kd/dot_general | solution.py:77
  203.6 8.8 %fusion.64 = (f32[2,512]{1,0:T(2,128)S(1)}, f32[2,512,2048]{2,1,0:T(8,128)}) fusion(pred[512,2048]{1,0:T(8,128)(4,1)S(1)} %fusion.63, bf16[2048,128]{1,0:T(8,128)(2,1)} %get-tuple-element.286, bf16[2048,2,128]{0,2,1:T(8,128)(2,1)} %get-tuple-element.285, s32[]{:T(128)S(6)} %select_n.57), kind=kOutput, calls=%fused_computation.47.clone.1 | convolution fusion | flops 547358720 | bytes 11276292 | tf_op jit(solution)/shard_map/while/body/eval_jaxpr/sub | solution.py:75
  212.4 6.2 %fusion.65 = f32[2048,128]{1,0:T(8,128)} fusion(f32[2,512,2048]{2,1,0:T(8,128)} %get-tuple-element.257, f32[2,512]{1,0:T(2,128)S(1)} %get-tuple-element.258, f32[2048,128]{1,0:T(8,128)} %get-tuple-element.271, pred[]{:T(512)S(6)} %compare.5, bf16[2048,2,128]{0,2,1:T(8,128)(2,1)S(1)} %get-tuple-element.287, s32[]{:T(128)S(6)} %select_n.57), kind=kOutput, calls=%fused_computation.16.clone.1 | convolution fusion | flops 541589504 | bytes 10752005 | tf_op jit(solution)/shard_map/while/body/eval_jaxpr/hqk,qhd->kd/dot_general | solution.py:77
  219.9 42.4 %all_to_all.42 = bf16[16,128,128]{2,1,0:T(8,128)(2,1)S(1)} all-to-all(bf16[16,128,128]{2,1,0:T(8,128)(2,1)S(1)} %bitcast.80), channel_id=1, replica_groups=mesh['seq'=16,'section'=8,'dp'=4] {'seq'}, dimensions={0} | all-to-all | bytes 1048576 | tf_op jit(solution)/shard_map/all_to_all | solution.py:84
  262.6 52.4 %all-gather.4.cloned.1.call-done = bf16[8192,576]{1,0:T(8,128)(2,1)} async-done(((bf16[128,576]{1,0:T(8,128)(2,1)}), bf16[8192,576]{1,0:T(8,128)(2,1)}) %all-gather.4.cloned.1.call-update) | async-done | bytes 9437200 | tf_op jit(solution)/shard_map/all_gather | solution.py:99
  315.0 8.8 %convolution_convert_fusion = bf16[128,8192]{1,0:T(8,128)(2,1)} fusion(bf16[8192,576]{1,0:T(8,128)(2,1)} %all-gather.4.cloned.1.call-done, bf16[128,64]{0,1:T(8,128)(2,1)S(1)} %convolution_convert_fusion.1, bf16[128,512]{0,1:T(8,128)(2,1)S(1)} %bitcast.78), kind=kOutput, calls=%fused_computation.30 | convolution fusion | flops 1209303040 | bytes 11681792 | tf_op jit(solution)/shard_map/dot_general | solution.py:97
  323.8 1.9 collective-permute-start
  327.9 255.9 %all-reduce.3.cloned.1.call-done = f32[64,512]{1,0:T(8,128)} async-done(((f32[64,512]{1,0:T(8,128)}), f32[64,512]{1,0:T(8,128)}) %all-reduce.3.cloned.1.call-update) | async-done | bytes 131088
  583.8 2.0 dynamic-slice_bitcast_fusion.1
  (53 shorter events, 14.7 us)
Async XLA Ops:
  7.2 255.3 %copy-start = (bf16[1,64,512]{2,1,0:T(8,128)(2,1)S(1)}, bf16[1,64,512]{2,1,0:T(8,128)(2,1)}, u32[]{:S(2)}) copy-start(bf16[1,64,512]{2,1,0:T(8,128)(2,1)} %param.20) | copy-start | bytes 196612
  7.2 18.3 %copy-start.4 = (bf16[1,128,64]{1,2,0:T(8,128)(2,1)S(1)}, bf16[1,128,64]{1,2,0:T(8,128)(2,1)}, u32[]{:S(2)}) copy-start(bf16[1,128,64]{1,2,0:T(8,128)(2,1)} %param.19) | copy-start | bytes 49156
  7.2 18.4 %copy-start.3 = (bf16[1,128,512]{2,1,0:T(8,128)(2,1)S(1)}, bf16[1,128,512]{2,1,0:T(8,128)(2,1)}, u32[]{:S(2)}) copy-start(bf16[1,128,512]{2,1,0:T(8,128)(2,1)} %param.18) | copy-start | bytes 393220
  7.2 19.1 %copy-start.1 = (bf16[1,1,128,4096]{3,2,1,0:T(8,128)(2,1)S(1)}, bf16[1,1,128,4096]{3,2,1,0:T(8,128)(2,1)}, u32[]{:S(2)}) copy-start(bf16[1,1,128,4096]{3,2,1,0:T(8,128)(2,1)} %param.12) | copy-start | bytes 3145732
  7.2 145.2 %all-gather.6.cloned.1.call-start = ((), (), s32[]{:S(2)}) async-start(), calls=%async_computation.4 | async-start | bytes 2228224 | tf_op jit(solution)/shard_map/all_gather | solution.py:51
  7.9 85.1 %copy-start.6 = (s32[1,1,2048]{2,1,0:T(1,128)S(1)}, s32[1,1,2048]{2,1,0:T(1,128)}, u32[]{:S(2)}) copy-start(s32[1,1,2048]{2,1,0:T(1,128)} %param.16) | copy-start | bytes 24580
  8.0 85.1 %copy-start.2 = (s32[1,1,2048]{2,1,0:T(1,128)S(1)}, s32[1,1,2048]{2,1,0:T(1,128)}, u32[]{:S(2)}) copy-start(s32[1,1,2048]{2,1,0:T(1,128)} %param.15) | copy-start | bytes 24580
  8.0 85.1 %copy-start.7 = (f32[1,1,16]{2,1,0:T(1,128)S(1)}, f32[1,1,16]{2,1,0:T(1,128)}, u32[]{:S(2)}) copy-start(f32[1,1,16]{2,1,0:T(1,128)} %param.17) | copy-start | bytes 196
  10.3 73.5 %all-to-all-start.1 = ((bf16[128,16,256]{0,2,1:T(8,128)(2,1)}), bf16[128,16,256]{0,2,1:T(8,128)(2,1)S(1)}, u32[]{:S(2)}, u32[]{:S(2)}) async-start(bf16[128,16,256]{0,2,1:T(8,128)(2,1)} %bitcast.4), calls=%async_computation.1 | async-start | bytes 2097152 | tf_op jit(solution)/shard_map/all_to_all | solution.py:48
  25.5 289.5 %all-gather.4.cloned.1.call-start = ((), (), s32[]{:S(2)}) async-start(), calls=%async_computation.3 | async-start | bytes 10649600 | tf_op jit(solution)/shard_map/all_gather | solution.py:99
  83.8 64.6 %all-to-all-start = ((bf16[128,16,256]{0,2,1:T(8,128)(2,1)}), bf16[128,16,256]{0,2,1:T(8,128)(2,1)S(1)}, u32[]{:S(2)}, u32[]{:S(2)}) async-start(bf16[128,16,256]{0,2,1:T(8,128)(2,1)} %bitcast.1), calls=%async_computation | async-start | bytes 2097152 | tf_op jit(solution)/shard_map/all_to_all | solution.py:47
  93.0 490.8 %all-reduce.3.cloned.1.call-start = ((), (), s32[]{:S(2)}) async-start(), calls=%async_computation.5 | async-start | bytes 262144
  262.6 63.1 %copy-start.5 = (bf16[1,1,128,64]{2,3,1,0:T(8,128)(2,1)S(1)}, bf16[1,1,128,64]{2,3,1,0:T(8,128)(2,1)}, u32[]{:S(2)}) copy-start(bf16[1,1,128,64]{2,3,1,0:T(8,128)(2,1)} %param.21) | copy-start | bytes 49156
  323.8 262.0 %collective-permute-start = (bf16[128,8192]{1,0:T(8,128)(2,1)}, bf16[128,8192]{1,0:T(8,128)(2,1)S(1)}, u32[]{:S(2)}, u32[]{:S(2)}) collective-permute-start(bf16[128,8192]{1,0:T(8,128)(2,1)} %convolution_convert_fusion), channel_id=1, source_target_pairs={{4,0},{8,4},{12,8},{16,12},{20,16},{24,20},{28,24},{5,1},{9,5},{13... | collective-permute-start | bytes 6291464 | tf_op jit(solution)/shard_map/ppermute | solution.py:15
Sparse Core Ops, SparseCore 0:
  10.1 131.3 all-gather.5
  144.5 170.4 all-gather.3
  326.7 257.0 all-reduce.2
where the time goes:
time: 594 us
  waiting for transfers between devices  416 us (70%)
  matrix products  69.5 us (12%)
  blocking collectives  42.4 us (7%)
  starting transfers between devices  26.4 us (4%)
  local copies, waits for them, and re-layouts  18.9 us (3%)
  between operations  14 us (2%)
  other arithmetic  6.59 us (1%)
    unnamed x4, waiting for transfers between devices  257 us
    all_to_all x1, waiting for transfers between devices, local(): lax.all_to_all(output_gradient[0, 0], 'seq', split_axis=1, concat_axis=0,...  56.1 us
    all_gather x1, waiting for transfers between devices, local(): lax.all_gather(weight_joined, ('seq', 'dp'), axis=0, tiled=True)  52.4 us
    all_to_all x1, waiting for transfers between devices, local(): lax.all_to_all(queries[0, 0], 'seq', split_axis=1, concat_axis=0, tiled=T...  50.7 us
    all_to_all x1, blocking collectives, local(): lax.all_to_all(value_part.astype(jnp.bfloat16), 'seq', split_axis=0, conc...  42.4 us
    sub x4, matrix products, add_block(): exp_terms = jnp.where(allowed[None], jnp.exp(scores - row_max), 0.0)  35.2 us
    dot_general x4, matrix products, add_block(): jnp.einsum('hqk,qhd->kd', prob_bf, grad_block, preferred_element_type=jnp...  24.5 us
    all_to_all x1, starting transfers between devices, local(): lax.all_to_all(output_gradient[0, 0], 'seq', split_axis=1, concat_axis=0,...  15.2 us
  transfers between devices with their start and end apart: 6, of which 4 were waited for; matrix products, arithmetic and copies ran while one was open for 14% of the time, Pallas kernels for 0%

commit v1 on v0

v1 whole, which is shorter than its diff:
```python
import functools
import jax
import jax.numpy as jnp
from jax import lax
from jax.experimental import pallas as pl
from jax.experimental.pallas import tpu as pltpu
from jax.sharding import PartitionSpec as P

HEAD_SIZE = 128
LONGEST = 384
NEG_FILL = -1e30
SCORE_SCALE = HEAD_SIZE ** (-0.5) * 1.4426950408889634


def shifted(value, moves, cyclic=()):
    axes = tuple(moves)
    sizes = [lax.axis_size(axis) for axis in axes]
    pairs = []
    total = 1
    for size in sizes:
        total *= size
    for source in range(total):
        rest, coords = source, []
        for size in reversed(sizes):
            coords.append(rest % size)
            rest //= size
        coords.reverse()
        target, inside = 0, True
        for axis, size, at in zip(axes, sizes, coords):
            to = at + moves[axis]
            if axis in cyclic:
                to %= size
            inside = inside and 0 <= to < size
            target = target * size + to
        if inside:
            pairs.append((source, target))
    return lax.ppermute(value, axes if len(axes) > 1 else axes[0], pairs)


def attention_kernel(q_ref, g_ref, w_ref, bias_ref, *refs, chunks, heads):
    key_refs, out_refs = refs[:chunks], refs[chunks:]
    rows = q_ref.shape[0]
    keys = jnp.concatenate([ref[:rows] for ref in key_refs], axis=0)
    bias = bias_ref[...]
    bias2 = jnp.concatenate([bias, bias], axis=1)
    weight = w_ref[...]
    total = None
    for pair in range(heads // 2):
        cols = [slice((2 * pair + k) * HEAD_SIZE, (2 * pair + k + 1) * HEAD_SIZE) for k in (0, 1)]
        q2 = jnp.concatenate([q_ref[:, c] for c in cols], axis=0)
        g2 = jnp.concatenate(
            [(g_ref[:, c].astype(jnp.float32) * weight).astype(jnp.bfloat16) for c in cols], axis=0
        )
        scores = lax.dot_general(
            keys, q2, (((1,), (1,)), ((), ())), preferred_element_type=jnp.float32
        )
        scores = scores * SCORE_SCALE + bias2
        top = jnp.max(scores, axis=0, keepdims=True)
        terms = jnp.exp2(scores - top)
        inverse = 1.0 / jnp.sum(terms, axis=0, keepdims=True)
        probs = (terms * inverse).astype(jnp.bfloat16)
        part = jnp.dot(probs, g2, preferred_element_type=jnp.float32)
        total = part if total is None else total + part
    for index, ref in enumerate(out_refs):
        ref[...] = total[index * rows : (index + 1) * rows].astype(ref.dtype)


def attention(queries, grads, weight, bias, key_chunks):
    rows, width = queries.shape
    chunks = len(key_chunks)
    kv_heads = key_chunks[0].shape[1] // HEAD_SIZE
    group = width // kv_heads
    wide = pl.BlockSpec((rows, group), lambda i: (0, i))
    narrow = pl.BlockSpec((rows, HEAD_SIZE), lambda i: (0, i))
    keyed = pl.BlockSpec((key_chunks[0].shape[0], HEAD_SIZE), lambda i: (0, i))
    whole = lambda array: pl.BlockSpec(array.shape, lambda i: (0, 0))
    return pl.pallas_call(
        functools.partial(attention_kernel, chunks=chunks, heads=group // HEAD_SIZE),
        grid=(kv_heads,),
        in_specs=[wide, wide, whole(weight), whole(bias)] + [keyed] * chunks,
        out_specs=[narrow] * chunks,
        out_shape=[jax.ShapeDtypeStruct((rows, kv_heads * HEAD_SIZE), jnp.bfloat16)] * chunks,
        compiler_params=pltpu.CompilerParams(vmem_limit_bytes=32 * 1024 * 1024),
        cost_estimate=pl.CostEstimate(
            flops=4 * chunks * rows * rows * width,
            bytes_accessed=4 * rows * width,
            transcendentals=chunks * rows * rows * width // HEAD_SIZE,
        ),
    )(queries, grads, weight, bias, *key_chunks)


def packed_rows(array, width):
    bands = width // array.shape[1]
    rows = array.shape[0] // bands
    return jnp.concatenate([array[k * rows : (k + 1) * rows] for k in range(bands)], axis=1)


def prepare_kernel(keys_ref, act_ref, packed_ref):
    rows = keys_ref.shape[0]
    packed_ref[:rows] = keys_ref[...]
    packed_ref[rows:] = packed_rows(act_ref[...], keys_ref.shape[1])


def prepared(keys, act):
    extra = act.shape[0] * act.shape[1] // keys.shape[1]
    return pl.pallas_call(
        prepare_kernel,
        out_shape=jax.ShapeDtypeStruct((keys.shape[0] + extra, keys.shape[1]), keys.dtype),
        compiler_params=pltpu.CompilerParams(vmem_limit_bytes=32 * 1024 * 1024),
    )(keys, act)


def adapter_kernel(*refs, chunks):
    packed_refs, part_refs, out_ref = refs[:chunks], refs[chunks : 2 * chunks], refs[-1]
    members, count, width = out_ref.shape
    rank = members * count
    rows = part_refs[0].shape[0]
    act = jnp.concatenate(
        [
            ref[rows:, k * rank : (k + 1) * rank]
            for ref in packed_refs
            for k in range(width // rank)
        ],
        axis=0,
    )
    source = lax.broadcasted_iota(jnp.int32, (rank, rank), 0)
    target = lax.broadcasted_iota(jnp.int32, (rank, rank), 1)
    order = source == (target % count) * members + target // count
    order = order.astype(jnp.float32).astype(jnp.bfloat16)
    act = jnp.dot(act, order, preferred_element_type=jnp.float32).astype(jnp.bfloat16)
    parts = jnp.concatenate([ref[...] for ref in part_refs], axis=0)
    term = lax.dot_general(
        act, parts, (((0,), (0,)), ((), ())), preferred_element_type=jnp.float32
    )
    out_ref[...] = term.astype(out_ref.dtype).reshape(members, count, width)


def adapter_terms(packed_chunks, parts, members, seq_count):
    return pl.pallas_call(
        functools.partial(adapter_kernel, chunks=len(parts)),
        out_shape=jax.ShapeDtypeStruct((members, seq_count, parts[0].shape[1]), parts[0].dtype),
        compiler_params=pltpu.CompilerParams(vmem_limit_bytes=32 * 1024 * 1024),
    )(*packed_chunks, *parts)


def summed_kernel(*refs):
    part_refs, terms_ref, out_ref = refs[:-2], refs[-2], refs[-1]
    rows = part_refs[0].shape[0]
    total = part_refs[0][...].astype(jnp.float32)
    for ref in part_refs[1:]:
        total = total + ref[...].astype(jnp.float32)
    total = total.astype(out_ref.dtype)
    for member in range(out_ref.shape[0]):
        out_ref[member, :rows] = total
        out_ref[member, rows:] = terms_ref[member]


def summed_copies(parts, terms):
    rows, width = parts[0].shape
    members, extra, _ = terms.shape
    return pl.pallas_call(
        summed_kernel,
        out_shape=jax.ShapeDtypeStruct((members, rows + extra, width), parts[0].dtype),
        compiler_params=pltpu.CompilerParams(vmem_limit_bytes=32 * 1024 * 1024),
    )(*parts, terms)


def stacked_kernel(*refs):
    out_ref, start = refs[-1], 0
    for ref in refs[:-1]:
        out_ref[start : start + ref.shape[0]] = ref[...]
        start += ref.shape[0]


def stacked(arrays):
    rows = sum(array.shape[0] for array in arrays)
    return pl.pallas_call(
        stacked_kernel,
        out_shape=jax.ShapeDtypeStruct((rows, arrays[0].shape[1]), arrays[0].dtype),
        compiler_params=pltpu.CompilerParams(vmem_limit_bytes=32 * 1024 * 1024),
    )(*arrays)


def product_kernel(at_ref, grads_ref, *refs, distances, count):
    weight_refs, out_ref = refs[:-1], refs[-1]
    members, _, width = grads_ref.shape
    _, _, rows, block_rows = out_ref.shape
    grads = grads_ref[:, :rows].reshape(members * rows, width)
    at = at_ref[0]
    for ref, own in zip(weight_refs, distances):
        for first in range(0, len(own), 2):
            weights = ref[first * block_rows : (first + 2) * block_rows, :]
            values = lax.dot_general(
                grads, weights, (((1,), (1,)), ((), ())), preferred_element_type=jnp.float32
            ).astype(out_ref.dtype)
            for k in (0, 1):
                block = lax.rem(at + own[first + k], count)
                part = values[:, k * block_rows : (k + 1) * block_rows]
                out_ref[:, block] = part.reshape(members, rows, block_rows)


def products(at, grads, weights, distances, rows, block_rows, count):
    members = grads.shape[0]
    vmem = pl.BlockSpec(memory_space=pltpu.VMEM)
    return pl.pallas_call(
        functools.partial(product_kernel, distances=distances, count=count),
        in_specs=[pl.BlockSpec(memory_space=pltpu.SMEM)] + [vmem] * (1 + len(weights)),
        out_specs=vmem,
        out_shape=jax.ShapeDtypeStruct((members, count, rows, block_rows), grads.dtype),
        compiler_params=pltpu.CompilerParams(vmem_limit_bytes=48 * 1024 * 1024),
    )(at, grads, *weights)


def ordered_kernel(in_ref, out_ref):
    members, blocks, _, size = in_ref.shape
    for block in range(blocks):
        for member in range(members):
            at = (block * members + member) * size
            out_ref[:, at : at + size] = in_ref[member, block]


def ordered(exchanged):
    members, count, rows, size = exchanged.shape
    blocks = 2
    return pl.pallas_call(
        ordered_kernel,
        grid=(count // blocks,),
        in_specs=[pl.BlockSpec((members, blocks, rows, size), lambda i: (0, i, 0, 0))],
        out_specs=pl.BlockSpec((rows, blocks * members * size), lambda i: (0, i)),
        out_shape=jax.ShapeDtypeStruct((rows, count * members * size), exchanged.dtype),
        compiler_params=pltpu.CompilerParams(vmem_limit_bytes=32 * 1024 * 1024),
    )(exchanged)


def swapped(value, axis, bit):
    pairs = [(at, at ^ bit) for at in range(lax.axis_size(axis))]
    return lax.ppermute(value, axis, pairs)


def tied(values, others):
    return lax.optimization_barrier((values, others))[0]


def local(
    queries,
    keys,
    output_gradient,
    rollout_index,
    loss_token_mask,
    advantages,
    value_projection,
    adapter_down_weight,
    adapter_up_weight,
    adapter_activation,
):
    seq_at = lax.axis_index("seq")
    seq_count = lax.axis_size("seq")
    dp_count = lax.axis_size("dp")
    rows = queries.shape[2]
    rank = adapter_activation.shape[3]
    halo = min(-(-(LONGEST - 1) // rows), seq_count - 1)
    ring = functools.partial(shifted, cyclic=("seq",))

    packed = prepared(keys[0, 0], adapter_activation[0, 0])
    chunks = [shifted(packed, {"seq": d}) for d in range(halo, 0, -1)] + [packed]

    merged = (
        value_projection[0].astype(jnp.float32)
        + jnp.dot(adapter_down_weight[0], adapter_up_weight[0], preferred_element_type=jnp.float32)
    ).astype(jnp.bfloat16)
    block_rows = merged.shape[0]
    high4 = ring(merged, {"seq": -4, "section": -1})
    low4 = ring(merged, {"seq": 4, "section": -1})
    own = shifted(merged, {"section": -1})

    rollout_row = rollout_index[0, 0]
    start = seq_at * rows
    padded = jnp.concatenate([jnp.full((halo * rows,), -1, jnp.int32), rollout_row])
    window = lax.dynamic_slice_in_dim(padded, start, (halo + 1) * rows, 0)
    own_rollout = window[halo * rows :]
    own_mask = lax.dynamic_slice_in_dim(loss_token_mask[0, 0], start, rows, 0)
    advantage_values = advantages[0, 0]
    onehot = (
        own_rollout[:, None] == jnp.arange(advantage_values.shape[0], dtype=jnp.int32)[None, :]
    ).astype(jnp.float32)
    weight = jnp.sum(onehot * advantage_values[None, :], axis=1) * own_mask.astype(jnp.float32)
    weight = jnp.broadcast_to(weight[:, None], (rows, HEAD_SIZE))
    key_pos = jnp.arange((halo + 1) * rows, dtype=jnp.int32)
    row_pos = jnp.arange(rows, dtype=jnp.int32) + halo * rows
    allowed = (key_pos[:, None] <= row_pos[None, :]) & (window[:, None] == own_rollout[None, :])
    bias = jnp.where(allowed, 0.0, NEG_FILL).astype(jnp.float32)

    parts = attention(queries[0, 0], output_gradient[0, 0], weight, bias, chunks)

    returned = [
        shifted(part, {"seq": index - halo, "section": -1} if index < halo else {"section": -1})
        for index, part in enumerate(parts)
    ]
    terms = adapter_terms(chunks, parts, dp_count, seq_count)

    high4 = tied(high4, parts)
    far = ring(high4, {"seq": -4})
    far = tied(far, returned[-1])
    fours = stacked([own, high4, far, low4])
    before = ring(fours, {"seq": 1})
    after = ring(fours, {"seq": -1})
    two_before = ring(fours[: 2 * block_rows], {"seq": 2})
    two_after = ring(fours[block_rows : 3 * block_rows], {"seq": -2})

    copies = summed_copies(returned, terms)
    grads = lax.all_to_all(copies, "dp", split_axis=0, concat_axis=0, tiled=True)
    product = products(
        seq_at.astype(jnp.int32).reshape(1),
        grads,
        [fours, before, after, two_before, two_after],
        [(0, 4, 8, 12), (15, 3, 7, 11), (1, 5, 9, 13), (14, 2), (6, 10)],
        rows,
        block_rows,
        seq_count,
    )
    exchanged = lax.all_to_all(product, "dp", split_axis=0, concat_axis=0, tiled=True)
    handed = ordered(exchanged)

    term = jnp.sum(grads[:, rows:].astype(jnp.float32), axis=0)
    term = tied(term, product)
    bit = 1
    while bit < seq_count:
        term = term + swapped(term, "seq", bit)
        bit *= 2
    term = lax.dynamic_slice_in_dim(term, seq_at, 1, 0)
    return (handed[None, None], term[None])


def solution(mesh):
    placed = (
        P("section", "dp", "seq", None),
        P("section", "dp", "seq", None),
        P("section", "dp", "seq", None),
        P("section", "dp", None),
        P("section", "dp", None),
        P("section", "dp", None),
        P("section", ("seq", "dp"), None),
        P("section", ("seq", "dp"), None),
        P("section", None, None),
        P("section", "dp", "seq", None),
    )
    return jax.shard_map(
        local,
        mesh=mesh,
        in_specs=placed,
        out_specs=(P("section", "dp", "seq", None), P("section", ("seq", "dp"), None)),
        check_vma=False,
    )
```

time: 594 us -> 154 us (0.26)
  the two profiles are of different devices: /device:TPU:4 before, /device:TPU:12 now
where the time goes in v1:
time: 154 us; the launch traced here: 153 us
  starting transfers between devices  89.2 us (58%)
  waiting for transfers between devices  41.6 us (27%)
  Pallas kernels  12.9 us (8%)
  local copies, waits for them, and re-layouts  5.12 us (3%)
  other arithmetic  2.15 us (1%)
    ppermute x15, starting transfers between devices, shifted(): return lax.ppermute(value, axes if len(axes) > 1 else axes[0], pairs)  56.6 us
    ppermute x15, waiting for transfers between devices, shifted(): return lax.ppermute(value, axes if len(axes) > 1 else axes[0], pairs)  26.9 us
    ppermute x4, starting transfers between devices, swapped(): return lax.ppermute(value, axis, pairs)  23 us
    ppermute x4, waiting for transfers between devices, swapped(): return lax.ppermute(value, axis, pairs)  14.7 us
    pallas_call x1, Pallas kernels, attention(): pl.pallas_call(functools.partial(attention_kernel, chunks=chunks, heads=g...  5.41 us
    all_to_all x1, starting transfers between devices, local(): lax.all_to_all(copies, 'dp', split_axis=0, concat_axis=0, tiled=True)  4.91 us
    all_to_all x1, starting transfers between devices, local(): lax.all_to_all(product, 'dp', split_axis=0, concat_axis=0, tiled=True)  4.79 us
    unnamed x9, local copies, waits for them, and re-layouts  4.23 us
  transfers between devices with their start and end apart: 21, of which 9 were waited for; matrix products, arithmetic and copies ran while one was open for 3% of the time, Pallas kernels for 4%

profile of v1, /device:TPU:12, one launch (start us, length us, event | category | flops | bytes accessed | tf_op | source)
XLA Modules:
  0.0 153.0 jit_solution(10992082273261378912)
XLA Ops:
  2.5 6.5 %collective-permute-start = (bf16[144,512]{1,0:T(8,128)(2,1)S(1)}, bf16[144,512]{1,0:T(8,128)(2,1)S(1)}, u32[]{:S(2)}, u32[]{:S(2)}) collective-permute-start(bf16[144,512]{1,0:T(8,128)(2,1)S(1)} %shard_map.113.refs_3_), channel_id=1, source_target_pairs={{0,96},{32,128},{64,160},{96,192},{128,224},{160,256},{192,288},{2... | collective-permute-start | bytes 442376 | tf_op jit(solution)/shard_map/ppermute | solution.py:37
  9.0 6.4 %collective-permute-start.1 = (bf16[144,512]{1,0:T(8,128)(2,1)S(1)}, bf16[144,512]{1,0:T(8,128)(2,1)S(1)}, u32[]{:S(2)}, u32[]{:S(2)}) collective-permute-start(bf16[144,512]{1,0:T(8,128)(2,1)S(1)} %shard_map.113.refs_3_), channel_id=1, source_target_pairs={{0,64},{32,96},{64,128},{96,160},{128,192},{160,224},{192,256},{22... | collective-permute-start | bytes 442376 | tf_op jit(solution)/shard_map/ppermute | solution.py:37
  15.4 3.8 %collective-permute-start.2 = (bf16[144,512]{1,0:T(8,128)(2,1)S(1)}, bf16[144,512]{1,0:T(8,128)(2,1)S(1)}, u32[]{:S(2)}, u32[]{:S(2)}) collective-permute-start(bf16[144,512]{1,0:T(8,128)(2,1)S(1)} %shard_map.113.refs_3_), channel_id=1, source_target_pairs={{0,32},{32,64},{64,96},{96,128},{128,160},{160,192},{192,224},{224... | collective-permute-start | bytes 442376 | tf_op jit(solution)/shard_map/ppermute | solution.py:37
  20.4 2.8 %collective-permute-start.8 = (bf16[128,512]{1,0:T(8,128)(2,1)S(1)}, bf16[128,512]{1,0:T(8,128)(2,1)S(1)}, u32[]{:S(2)}, u32[]{:S(2)}) collective-permute-start(bf16[128,512]{1,0:T(8,128)(2,1)S(1)} %fusion), channel_id=1, source_target_pairs={{4,384},{8,388},{12,392},{16,396},{20,400},{24,404},{28,408},{36,4... | collective-permute-start | bytes 393224 | tf_op jit(solution)/shard_map/ppermute | solution.py:37
  28.1 5.4 %shard_map.114 = (bf16[128,512]{1,0:T(8,128)(2,1)S(1)}, bf16[128,512]{1,0:T(8,128)(2,1)S(1)}, bf16[128,512]{1,0:T(8,128)(2,1)S(1)}, bf16[128,512]{1,0:T(8,128)(2,1)S(1)}) custom-call(bf16[128,4096]{1,0:T(8,128)(2,1)S(1)} %bitcast.25, bf16[128,4096]{1,0:T(8,128)(2,1)S(1)} %bitcast.26, f32[128,128]{1,0:T(8,128)S(1)} %broadcast_in_dim.12.w_ref, ...), custom_call_target="tpu_custom_call" | custom-call | flops 1073741824 | bytes 2097152 | tf_op jit(solution)/shard_map/pallas_call | solution.py:77
  33.5 3.3 %collective-permute-done.8.refs_1_ = bf16[128,512]{1,0:T(8,128)(2,1)S(1)} collective-permute-done((bf16[128,512]{1,0:T(8,128)(2,1)S(1)}, bf16[128,512]{1,0:T(8,128)(2,1)S(1)}, u32[]{:S(2)}, u32[]{:S(2)}) %collective-permute-start.8) | collective-permute-done | bytes 131104 | tf_op jit(solution)/shard_map/ppermute | solution.py:37
  36.8 11.8 %collective-permute-start.9 = (bf16[128,512]{1,0:T(8,128)(2,1)S(1)}, bf16[128,512]{1,0:T(8,128)(2,1)S(1)}, u32[]{:S(2)}, u32[]{:S(2)}) collective-permute-start(bf16[128,512]{1,0:T(8,128)(2,1)S(1)} %collective-permute-done.8.refs_1_), channel_id=1, source_target_pairs={{0,384},{32,416},{64,448},{96,480},{128,0},{160,32},{192,64},{224,... | collective-permute-start | bytes 393224 | tf_op jit(solution)/shard_map/ppermute | solution.py:37
  56.3 2.9 %collective-permute-done.9.refs_2_ = bf16[128,512]{1,0:T(8,128)(2,1)S(1)} collective-permute-done((bf16[128,512]{1,0:T(8,128)(2,1)S(1)}, bf16[128,512]{1,0:T(8,128)(2,1)S(1)}, u32[]{:S(2)}, u32[]{:S(2)}) %collective-permute-start.9) | collective-permute-done | bytes 131104 | tf_op jit(solution)/shard_map/ppermute | solution.py:37
  61.8 8.2 %collective-permute-done.10.refs_3_ = bf16[128,512]{1,0:T(8,128)(2,1)S(1)} collective-permute-done((bf16[128,512]{1,0:T(8,128)(2,1)S(1)}, bf16[128,512]{1,0:T(8,128)(2,1)S(1)}, u32[]{:S(2)}, u32[]{:S(2)}) %collective-permute-start.10) | collective-permute-done | bytes 131104 | tf_op jit(solution)/shard_map/ppermute | solution.py:37
  72.0 5.1 %collective-permute-start.12 = (bf16[512,512]{1,0:T(8,128)(2,1)S(1)}, bf16[512,512]{1,0:T(8,128)(2,1)S(1)}, u32[]{:S(2)}, u32[]{:S(2)}) collective-permute-start(bf16[512,512]{1,0:T(8,128)(2,1)S(1)} %shard_map.117.refs_0_), channel_id=1, source_target_pairs={{0,480},{32,0},{64,32},{96,64},{128,96},{160,128},{192,160},{224,1... | collective-permute-start | bytes 1572872 | tf_op jit(solution)/shard_map/ppermute | solution.py:37
  78.5 4.9 %all-to-all-start = ((bf16[4,144,512]{2,1,0:T(8,128)(2,1)}), bf16[4,144,512]{2,1,0:T(8,128)(2,1)S(1)}, u32[]{:S(2)}, u32[]{:S(2)}) async-start(bf16[4,144,512]{2,1,0:T(8,128)(2,1)} %shard_map.116), calls=%async_computation | async-start | bytes 1179648 | tf_op jit(solution)/shard_map/all_to_all | solution.py:311
  83.4 3.5 %collective-permute-start.13 = (bf16[256,512]{1,0:T(8,128)(2,1)S(1)}, bf16[256,512]{1,0:T(8,128)(2,1)S(1)}, u32[]{:S(2)}, u32[]{:S(2)}) collective-permute-start(bf16[256,512]{1,0:T(8,128)(2,1)S(1)} %get-tuple-element.17), channel_id=1, source_target_pairs={{0,64},{32,96},{64,128},{96,160},{128,192},{160,224},{192,256},{22... | collective-permute-start | bytes 786440 | tf_op jit(solution)/shard_map/ppermute | solution.py:37
  86.9 4.5 %collective-permute-start.14 = (bf16[256,512]{1,0:T(8,128)(2,1)S(1)}, bf16[256,512]{1,0:T(8,128)(2,1)S(1)}, u32[]{:S(2)}, u32[]{:S(2)}) collective-permute-start(bf16[256,512]{1,0:T(8,128)(2,1)S(1)} %get-tuple-element.16), channel_id=1, source_target_pairs={{0,448},{32,480},{64,0},{96,32},{128,64},{160,96},{192,128},{224,1... | collective-permute-start | bytes 786440 | tf_op jit(solution)/shard_map/ppermute | solution.py:37
  91.4 9.2 %collective-permute-done.13.refs_3_ = bf16[256,512]{1,0:T(8,128)(2,1)S(1)} collective-permute-done((bf16[256,512]{1,0:T(8,128)(2,1)S(1)}, bf16[256,512]{1,0:T(8,128)(2,1)S(1)}, u32[]{:S(2)}, u32[]{:S(2)}) %collective-permute-start.13) | collective-permute-done | bytes 262176 | tf_op jit(solution)/shard_map/ppermute | solution.py:37
  100.6 3.4 %collective-permute-done.14.refs_4_ = bf16[256,512]{1,0:T(8,128)(2,1)S(1)} collective-permute-done((bf16[256,512]{1,0:T(8,128)(2,1)S(1)}, bf16[256,512]{1,0:T(8,128)(2,1)S(1)}, u32[]{:S(2)}, u32[]{:S(2)}) %collective-permute-start.14) | collective-permute-done | bytes 262176 | tf_op jit(solution)/shard_map/ppermute | solution.py:37
  103.9 2.8 %shard_map.118 = bf16[4,16,128,128]{3,2,1,0:T(8,128)(2,1)} custom-call(s32[1]{0:T(128)} %bitcast.at_ref, bf16[4,144,512]{2,1,0:T(8,128)(2,1)S(1)} %all-to-all-done.grads_ref, bf16[512,512]{1,0:T(8,128)(2,1)S(1)} %shard_map.117.refs_0_, bf16[512,512]{1,0:T(8,128)(2,1)S(1)} %collective-permute-done.11.refs_1_, ...), custom_call_target="tpu_custom_call" | custom-call | tf_op jit(solution)/shard_map/pallas_call | solution.py:205
  106.7 4.8 %all-to-all-start.1 = ((bf16[4,16,128,128]{3,2,1,0:T(8,128)(2,1)}), bf16[4,16,128,128]{3,2,1,0:T(8,128)(2,1)S(1)}, u32[]{:S(2)}, u32[]{:S(2)}) async-start(bf16[4,16,128,128]{3,2,1,0:T(8,128)(2,1)} %shard_map.118), calls=%async_computation.1 | async-start | bytes 4194304 | tf_op jit(solution)/shard_map/all_to_all | solution.py:321
  113.4 3.9 %collective-permute-done.15 = f32[16,512]{1,0:T(8,128)S(1)} collective-permute-done((f32[16,512]{1,0:T(8,128)S(1)}, f32[16,512]{1,0:T(8,128)S(1)}, u32[]{:S(2)}, u32[]{:S(2)}) %collective-permute-start.15) | collective-permute-done | bytes 32800 | tf_op jit(solution)/shard_map/ppermute | solution.py:237
  117.3 5.7 %collective-permute-start.16 = (f32[16,512]{1,0:T(8,128)S(1)}, f32[16,512]{1,0:T(8,128)S(1)}, u32[]{:S(2)}, u32[]{:S(2)}) collective-permute-start(f32[16,512]{1,0:T(8,128)S(1)} %add.41), channel_id=1, source_target_pairs={{0,64},{32,96},{64,0},{96,32},{128,192},{160,224},{192,128},{224,1... | collective-permute-start | bytes 98312 | tf_op jit(solution)/shard_map/ppermute | solution.py:237
  125.0 5.5 %collective-permute-start.17 = (f32[16,512]{1,0:T(8,128)S(1)}, f32[16,512]{1,0:T(8,128)S(1)}, u32[]{:S(2)}, u32[]{:S(2)}) collective-permute-start(f32[16,512]{1,0:T(8,128)S(1)} %add.42), channel_id=1, source_target_pairs={{0,128},{32,160},{64,192},{96,224},{128,0},{160,32},{192,64},{224,... | collective-permute-start | bytes 98312 | tf_op jit(solution)/shard_map/ppermute | solution.py:237
  130.5 4.2 %collective-permute-done.17 = f32[16,512]{1,0:T(8,128)S(1)} collective-permute-done((f32[16,512]{1,0:T(8,128)S(1)}, f32[16,512]{1,0:T(8,128)S(1)}, u32[]{:S(2)}, u32[]{:S(2)}) %collective-permute-start.17) | collective-permute-done | bytes 32800 | tf_op jit(solution)/shard_map/ppermute | solution.py:237
  134.7 9.8 %collective-permute-start.18 = (f32[16,512]{1,0:T(8,128)S(1)}, f32[16,512]{1,0:T(8,128)S(1)}, u32[]{:S(2)}, u32[]{:S(2)}) collective-permute-start(f32[16,512]{1,0:T(8,128)S(1)} %add.43), channel_id=1, source_target_pairs={{0,256},{32,288},{64,320},{96,352},{128,384},{160,416},{192,448},{... | collective-permute-start | bytes 98312 | tf_op jit(solution)/shard_map/ppermute | solution.py:237
  144.5 4.7 %collective-permute-done.18 = f32[16,512]{1,0:T(8,128)S(1)} collective-permute-done((f32[16,512]{1,0:T(8,128)S(1)}, f32[16,512]{1,0:T(8,128)S(1)}, u32[]{:S(2)}, u32[]{:S(2)}) %collective-permute-start.18) | collective-permute-done | bytes 32800 | tf_op jit(solution)/shard_map/ppermute | solution.py:237
  149.8 3.3 %shard_map.119 = bf16[128,8192]{1,0:T(8,128)(2,1)} custom-call(bf16[4,16,128,128]{3,2,1,0:T(8,128)(2,1)S(1)} %all-to-all-done.1.in_ref), custom_call_target="tpu_custom_call" | custom-call | tf_op jit(solution)/shard_map/pallas_call | solution.py:225
  (48 shorter events, 25.8 us)
Async XLA Ops:
  0.6 18.6 %copy-start = (bf16[1,64,512]{2,1,0:T(8,128)(2,1)S(1)}, bf16[1,64,512]{2,1,0:T(8,128)(2,1)}, u32[]{:S(2)}) copy-start(bf16[1,64,512]{2,1,0:T(8,128)(2,1)} %param.18) | copy-start | bytes 196612
  2.5 23.1 %collective-permute-start = (bf16[144,512]{1,0:T(8,128)(2,1)S(1)}, bf16[144,512]{1,0:T(8,128)(2,1)S(1)}, u32[]{:S(2)}, u32[]{:S(2)}) collective-permute-start(bf16[144,512]{1,0:T(8,128)(2,1)S(1)} %shard_map.113.refs_3_), channel_id=1, source_target_pairs={{0,96},{32,128},{64,160},{96,192},{128,224},{160,256},{192,288},{2... | collective-permute-start | bytes 442376 | tf_op jit(solution)/shard_map/ppermute | solution.py:37
  9.0 16.5 %collective-permute-start.1 = (bf16[144,512]{1,0:T(8,128)(2,1)S(1)}, bf16[144,512]{1,0:T(8,128)(2,1)S(1)}, u32[]{:S(2)}, u32[]{:S(2)}) collective-permute-start(bf16[144,512]{1,0:T(8,128)(2,1)S(1)} %shard_map.113.refs_3_), channel_id=1, source_target_pairs={{0,64},{32,96},{64,128},{96,160},{128,192},{160,224},{192,256},{22... | collective-permute-start | bytes 442376 | tf_op jit(solution)/shard_map/ppermute | solution.py:37
  15.4 10.1 %collective-permute-start.2 = (bf16[144,512]{1,0:T(8,128)(2,1)S(1)}, bf16[144,512]{1,0:T(8,128)(2,1)S(1)}, u32[]{:S(2)}, u32[]{:S(2)}) collective-permute-start(bf16[144,512]{1,0:T(8,128)(2,1)S(1)} %shard_map.113.refs_3_), channel_id=1, source_target_pairs={{0,32},{32,64},{64,96},{96,128},{128,160},{160,192},{192,224},{224... | collective-permute-start | bytes 442376 | tf_op jit(solution)/shard_map/ppermute | solution.py:37
  20.4 16.4 %collective-permute-start.8 = (bf16[128,512]{1,0:T(8,128)(2,1)S(1)}, bf16[128,512]{1,0:T(8,128)(2,1)S(1)}, u32[]{:S(2)}, u32[]{:S(2)}) collective-permute-start(bf16[128,512]{1,0:T(8,128)(2,1)S(1)} %fusion), channel_id=1, source_target_pairs={{4,384},{8,388},{12,392},{16,396},{20,400},{24,404},{28,408},{36,4... | collective-permute-start | bytes 393224 | tf_op jit(solution)/shard_map/ppermute | solution.py:37
  25.6 1.2 copy-start.2
  26.9 1.2 copy-start.3
  36.8 22.4 %collective-permute-start.9 = (bf16[128,512]{1,0:T(8,128)(2,1)S(1)}, bf16[128,512]{1,0:T(8,128)(2,1)S(1)}, u32[]{:S(2)}, u32[]{:S(2)}) collective-permute-start(bf16[128,512]{1,0:T(8,128)(2,1)S(1)} %collective-permute-done.8.refs_1_), channel_id=1, source_target_pairs={{0,384},{32,416},{64,448},{96,480},{128,0},{160,32},{192,64},{224,... | collective-permute-start | bytes 393224 | tf_op jit(solution)/shard_map/ppermute | solution.py:37
  48.6 11.9 %collective-permute-start.6 = (bf16[128,512]{1,0:T(8,128)(2,1)S(1)}, bf16[128,512]{1,0:T(8,128)(2,1)S(1)}, u32[]{:S(2)}, u32[]{:S(2)}) collective-permute-start(bf16[128,512]{1,0:T(8,128)(2,1)S(1)} %get-tuple-element.12.refs_7_), channel_id=1, source_target_pairs={{4,0},{8,4},{12,8},{16,12},{20,16},{24,20},{28,24},{5,1},{9,5},{13... | collective-permute-start | bytes 393224 | tf_op jit(solution)/shard_map/ppermute | solution.py:37
  50.5 19.5 %collective-permute-start.10 = (bf16[128,512]{1,0:T(8,128)(2,1)S(1)}, bf16[128,512]{1,0:T(8,128)(2,1)S(1)}, u32[]{:S(2)}, u32[]{:S(2)}) collective-permute-start(bf16[128,512]{1,0:T(8,128)(2,1)S(1)} %fusion), channel_id=1, source_target_pairs={{4,128},{8,132},{12,136},{16,140},{20,144},{24,148},{28,152},{36,1... | collective-permute-start | bytes 393224 | tf_op jit(solution)/shard_map/ppermute | solution.py:37
  52.4 17.6 %collective-permute-start.7 = (bf16[128,512]{1,0:T(8,128)(2,1)S(1)}, bf16[128,512]{1,0:T(8,128)(2,1)S(1)}, u32[]{:S(2)}, u32[]{:S(2)}) collective-permute-start(bf16[128,512]{1,0:T(8,128)(2,1)S(1)} %fusion), channel_id=1, source_target_pairs={{4,0},{8,4},{12,8},{16,12},{20,16},{24,20},{28,24},{5,1},{9,5},{13... | collective-permute-start | bytes 393224 | tf_op jit(solution)/shard_map/ppermute | solution.py:37
  55.0 22.6 %collective-permute-start.3 = (bf16[128,512]{1,0:T(8,128)(2,1)S(1)}, bf16[128,512]{1,0:T(8,128)(2,1)S(1)}, u32[]{:S(2)}, u32[]{:S(2)}) collective-permute-start(bf16[128,512]{1,0:T(8,128)(2,1)S(1)} %get-tuple-element.9.refs_4_), channel_id=1, source_target_pairs={{100,0},{104,4},{108,8},{112,12},{116,16},{120,20},{124,24},{132,3... | collective-permute-start | bytes 393224 | tf_op jit(solution)/shard_map/ppermute | solution.py:37
  59.2 18.4 %collective-permute-start.4 = (bf16[128,512]{1,0:T(8,128)(2,1)S(1)}, bf16[128,512]{1,0:T(8,128)(2,1)S(1)}, u32[]{:S(2)}, u32[]{:S(2)}) collective-permute-start(bf16[128,512]{1,0:T(8,128)(2,1)S(1)} %get-tuple-element.10.refs_5_), channel_id=1, source_target_pairs={{68,0},{72,4},{76,8},{80,12},{84,16},{88,20},{92,24},{100,32},{104... | collective-permute-start | bytes 393224 | tf_op jit(solution)/shard_map/ppermute | solution.py:37
  60.5 17.1 %collective-permute-start.5 = (bf16[128,512]{1,0:T(8,128)(2,1)S(1)}, bf16[128,512]{1,0:T(8,128)(2,1)S(1)}, u32[]{:S(2)}, u32[]{:S(2)}) collective-permute-start(bf16[128,512]{1,0:T(8,128)(2,1)S(1)} %get-tuple-element.11.refs_6_), channel_id=1, source_target_pairs={{36,0},{40,4},{44,8},{48,12},{52,16},{56,20},{60,24},{68,32},{72,3... | collective-permute-start | bytes 393224 | tf_op jit(solution)/shard_map/ppermute | solution.py:37
  70.0 33.9 %collective-permute-start.11 = (bf16[512,512]{1,0:T(8,128)(2,1)S(1)}, bf16[512,512]{1,0:T(8,128)(2,1)S(1)}, u32[]{:S(2)}, u32[]{:S(2)}) collective-permute-start(bf16[512,512]{1,0:T(8,128)(2,1)S(1)} %shard_map.117.refs_0_), channel_id=1, source_target_pairs={{0,32},{32,64},{64,96},{96,128},{128,160},{160,192},{192,224},{224... | collective-permute-start | bytes 1572872 | tf_op jit(solution)/shard_map/ppermute | solution.py:37
  72.0 32.0 %collective-permute-start.12 = (bf16[512,512]{1,0:T(8,128)(2,1)S(1)}, bf16[512,512]{1,0:T(8,128)(2,1)S(1)}, u32[]{:S(2)}, u32[]{:S(2)}) collective-permute-start(bf16[512,512]{1,0:T(8,128)(2,1)S(1)} %shard_map.117.refs_0_), channel_id=1, source_target_pairs={{0,480},{32,0},{64,32},{96,64},{128,96},{160,128},{192,160},{224,1... | collective-permute-start | bytes 1572872 | tf_op jit(solution)/shard_map/ppermute | solution.py:37
  78.5 25.4 %all-to-all-start = ((bf16[4,144,512]{2,1,0:T(8,128)(2,1)}), bf16[4,144,512]{2,1,0:T(8,128)(2,1)S(1)}, u32[]{:S(2)}, u32[]{:S(2)}) async-start(bf16[4,144,512]{2,1,0:T(8,128)(2,1)} %shard_map.116), calls=%async_computation | async-start | bytes 1179648 | tf_op jit(solution)/shard_map/all_to_all | solution.py:311
  83.4 17.1 %collective-permute-start.13 = (bf16[256,512]{1,0:T(8,128)(2,1)S(1)}, bf16[256,512]{1,0:T(8,128)(2,1)S(1)}, u32[]{:S(2)}, u32[]{:S(2)}) collective-permute-start(bf16[256,512]{1,0:T(8,128)(2,1)S(1)} %get-tuple-element.17), channel_id=1, source_target_pairs={{0,64},{32,96},{64,128},{96,160},{128,192},{160,224},{192,256},{22... | collective-permute-start | bytes 786440 | tf_op jit(solution)/shard_map/ppermute | solution.py:37
  86.9 17.0 %collective-permute-start.14 = (bf16[256,512]{1,0:T(8,128)(2,1)S(1)}, bf16[256,512]{1,0:T(8,128)(2,1)S(1)}, u32[]{:S(2)}, u32[]{:S(2)}) collective-permute-start(bf16[256,512]{1,0:T(8,128)(2,1)S(1)} %get-tuple-element.16), channel_id=1, source_target_pairs={{0,448},{32,480},{64,0},{96,32},{128,64},{160,96},{192,128},{224,1... | collective-permute-start | bytes 786440 | tf_op jit(solution)/shard_map/ppermute | solution.py:37
  106.7 43.1 %all-to-all-start.1 = ((bf16[4,16,128,128]{3,2,1,0:T(8,128)(2,1)}), bf16[4,16,128,128]{3,2,1,0:T(8,128)(2,1)S(1)}, u32[]{:S(2)}, u32[]{:S(2)}) async-start(bf16[4,16,128,128]{3,2,1,0:T(8,128)(2,1)} %shard_map.118), calls=%async_computation.1 | async-start | bytes 4194304 | tf_op jit(solution)/shard_map/all_to_all | solution.py:321
  111.5 5.8 %collective-permute-start.15 = (f32[16,512]{1,0:T(8,128)S(1)}, f32[16,512]{1,0:T(8,128)S(1)}, u32[]{:S(2)}, u32[]{:S(2)}) collective-permute-start(f32[16,512]{1,0:T(8,128)S(1)} %convert_reduce_fusion), channel_id=1, source_target_pairs={{0,32},{32,0},{64,96},{96,64},{128,160},{160,128},{192,224},{224,1... | collective-permute-start | bytes 98312 | tf_op jit(solution)/shard_map/ppermute | solution.py:237
  117.3 7.6 %collective-permute-start.16 = (f32[16,512]{1,0:T(8,128)S(1)}, f32[16,512]{1,0:T(8,128)S(1)}, u32[]{:S(2)}, u32[]{:S(2)}) collective-permute-start(f32[16,512]{1,0:T(8,128)S(1)} %add.41), channel_id=1, source_target_pairs={{0,64},{32,96},{64,0},{96,32},{128,192},{160,224},{192,128},{224,1... | collective-permute-start | bytes 98312 | tf_op jit(solution)/shard_map/ppermute | solution.py:237
  125.0 9.7 %collective-permute-start.17 = (f32[16,512]{1,0:T(8,128)S(1)}, f32[16,512]{1,0:T(8,128)S(1)}, u32[]{:S(2)}, u32[]{:S(2)}) collective-permute-start(f32[16,512]{1,0:T(8,128)S(1)} %add.42), channel_id=1, source_target_pairs={{0,128},{32,160},{64,192},{96,224},{128,0},{160,32},{192,64},{224,... | collective-permute-start | bytes 98312 | tf_op jit(solution)/shard_map/ppermute | solution.py:237
  134.7 14.5 %collective-permute-start.18 = (f32[16,512]{1,0:T(8,128)S(1)}, f32[16,512]{1,0:T(8,128)S(1)}, u32[]{:S(2)}, u32[]{:S(2)}) collective-permute-start(f32[16,512]{1,0:T(8,128)S(1)} %add.43), channel_id=1, source_target_pairs={{0,256},{32,288},{64,320},{96,352},{128,384},{160,416},{192,448},{... | collective-permute-start | bytes 98312 | tf_op jit(solution)/shard_map/ppermute | solution.py:237
  (1 other events, 0.9 us)

commit v2 on v1

--- a/solution.py
+++ b/solution.py
@@ -181,60 +181,74 @@
     )(*arrays)
 
 
-def product_kernel(at_ref, grads_ref, *refs, distances, count):
+def product_kernel(grads_ref, *refs):
     weight_refs, out_ref = refs[:-1], refs[-1]
     members, _, width = grads_ref.shape
     _, _, rows, block_rows = out_ref.shape
     grads = grads_ref[:, :rows].reshape(members * rows, width)
-    at = at_ref[0]
-    for ref, own in zip(weight_refs, distances):
-        for first in range(0, len(own), 2):
-            weights = ref[first * block_rows : (first + 2) * block_rows, :]
-            values = lax.dot_general(
-                grads, weights, (((1,), (1,)), ((), ())), preferred_element_type=jnp.float32
-            ).astype(out_ref.dtype)
-            for k in (0, 1):
-                block = lax.rem(at + own[first + k], count)
-                part = values[:, k * block_rows : (k + 1) * block_rows]
-                out_ref[:, block] = part.reshape(members, rows, block_rows)
-
-
-def products(at, grads, weights, distances, rows, block_rows, count):
-    members = grads.shape[0]
-    vmem = pl.BlockSpec(memory_space=pltpu.VMEM)
-    return pl.pallas_call(
-        functools.partial(product_kernel, distances=distances, count=count),
-        in_specs=[pl.BlockSpec(memory_space=pltpu.SMEM)] + [vmem] * (1 + len(weights)),
-        out_specs=vmem,
-        out_shape=jax.ShapeDtypeStruct((members, count, rows, block_rows), grads.dtype),
+    block = 0
+    for ref in weight_refs:
+        values = lax.dot_general(
+            grads, ref[...], (((1,), (1,)), ((), ())), preferred_element_type=jnp.float32
+        ).astype(out_ref.dtype)
+        for k in range(ref.shape[0] // block_rows):
+            part = values[:, k * block_rows : (k + 1) * block_rows]
+            out_ref[:, block] = part.reshape(members, rows, block_rows)
+            block += 1
+
+
+def products(grads, weights, rows, block_rows):
+    blocks = sum(weight.shape[0] for weight in weights) // block_rows
+    return pl.pallas_call(
+        product_kernel,
+        out_shape=jax.ShapeDtypeStruct((grads.shape[0], blocks, rows, block_rows), grads.dtype),
         compiler_params=pltpu.CompilerParams(vmem_limit_bytes=48 * 1024 * 1024),
-    )(at, grads, *weights)
-
-
-def ordered_kernel(in_ref, out_ref):
-    members, blocks, _, size = in_ref.shape
-    for block in range(blocks):
-        for member in range(members):
-            at = (block * members + member) * size
-            out_ref[:, at : at + size] = in_ref[member, block]
-
-
-def ordered(exchanged):
-    members, count, rows, size = exchanged.shape
-    blocks = 2
-    return pl.pallas_call(
-        ordered_kernel,
-        grid=(count // blocks,),
-        in_specs=[pl.BlockSpec((members, blocks, rows, size), lambda i: (0, i, 0, 0))],
-        out_specs=pl.BlockSpec((rows, blocks * members * size), lambda i: (0, i)),
+    )(grads, *weights)
+
+
+def placed_kernel(places_ref, in_ref, *refs):
+    out_ref = refs[-1]
+    members, _, _, size = in_ref.shape
+    for member in range(members):
+        out_ref[:, member * size : (member + 1) * size] = in_ref[member, 0]
+
+
+def placed_blocks(exchanged, places, count, before=None):
+    members, blocks, rows, size = exchanged.shape
+    operands = [exchanged] + ([] if before is None else [before])
+    return pl.pallas_call(
+        placed_kernel,
+        grid_spec=pltpu.PrefetchScalarGridSpec(
+            num_scalar_prefetch=1,
+            grid=(blocks,),
+            in_specs=[pl.BlockSpec((members, 1, rows, size), lambda i, places: (0, i, 0, 0))]
+            + ([] if before is None else [pl.BlockSpec(memory_space=pl.ANY)]),
+            out_specs=pl.BlockSpec((rows, members * size), lambda i, places: (0, places[i])),
+        ),
         out_shape=jax.ShapeDtypeStruct((rows, count * members * size), exchanged.dtype),
-        compiler_params=pltpu.CompilerParams(vmem_limit_bytes=32 * 1024 * 1024),
-    )(exchanged)
-
-
-def swapped(value, axis, bit):
-    pairs = [(at, at ^ bit) for at in range(lax.axis_size(axis))]
-    return lax.ppermute(value, axis, pairs)
+        input_output_aliases={} if before is None else {2: 0},
+        compiler_params=pltpu.CompilerParams(vmem_limit_bytes=32 * 1024 * 1024),
+    )(places, *operands)
+
+
+def term_kernel(grads_ref, out_ref):
+    total = grads_ref[0].astype(jnp.float32)
+    for member in range(1, grads_ref.shape[0]):
+        total = total + grads_ref[member].astype(jnp.float32)
+    out_ref[...] = total
+
+
+def summed_terms(grads, rows):
+    members, total, width = grads.shape
+    extra = total - rows
+    return pl.pallas_call(
+        term_kernel,
+        grid=(1,),
+        in_specs=[pl.BlockSpec((members, extra, width), lambda i: (0, rows // extra, 0))],
+        out_specs=pl.BlockSpec((extra, width), lambda i: (0, 0)),
+        out_shape=jax.ShapeDtypeStruct((extra, width), jnp.float32),
+        compiler_params=pltpu.CompilerParams(vmem_limit_bytes=32 * 1024 * 1024),
+    )(grads)
 
 
 def tied(values, others):
@@ -269,6 +283,7 @@
         + jnp.dot(adapter_down_weight[0], adapter_up_weight[0], preferred_element_type=jnp.float32)
     ).astype(jnp.bfloat16)
     block_rows = merged.shape[0]
+    merged = tied(merged, chunks[2])
     high4 = ring(merged, {"seq": -4, "section": -1})
     low4 = ring(merged, {"seq": 4, "section": -1})
     own = shifted(merged, {"section": -1})
@@ -298,36 +313,35 @@
     ]
     terms = adapter_terms(chunks, parts, dp_count, seq_count)
 
-    high4 = tied(high4, parts)
-    far = ring(high4, {"seq": -4})
+    high4, low4, own = tied([high4, low4, own], parts)
+    half = block_rows // 2
+    far = [ring(low4[:half], {"seq": 4}), ring(high4[half:], {"seq": -4})]
     far = tied(far, returned[-1])
-    fours = stacked([own, high4, far, low4])
-    before = ring(fours, {"seq": 1})
-    after = ring(fours, {"seq": -1})
-    two_before = ring(fours[: 2 * block_rows], {"seq": 2})
-    two_after = ring(fours[block_rows : 3 * block_rows], {"seq": -2})
+    held = stacked([own, high4] + far + [low4])
+    before = ring(held, {"seq": 1})
+    after = ring(held, {"seq": -1})
+    two_before = ring(before[: 2 * block_rows], {"seq": 1})
+    two_after = ring(after[block_rows : 3 * block_rows], {"seq": -1})
 
     copies = summed_copies(returned, terms)
     grads = lax.all_to_all(copies, "dp", split_axis=0, concat_axis=0, tiled=True)
-    product = products(
-        seq_at.astype(jnp.int32).reshape(1),
-        grads,
-        [fours, before, after, two_before, two_after],
-        [(0, 4, 8, 12), (15, 3, 7, 11), (1, 5, 9, 13), (14, 2), (6, 10)],
-        rows,
-        block_rows,
-        seq_count,
-    )
-    exchanged = lax.all_to_all(product, "dp", split_axis=0, concat_axis=0, tiled=True)
-    handed = ordered(exchanged)
-
-    term = jnp.sum(grads[:, rows:].astype(jnp.float32), axis=0)
-    term = tied(term, product)
-    bit = 1
-    while bit < seq_count:
-        term = term + swapped(term, "seq", bit)
-        bit *= 2
-    term = lax.dynamic_slice_in_dim(term, seq_at, 1, 0)
+    term = summed_terms(grads, rows)
+    term = term.reshape(seq_count, 1, -1)
+    term = lax.all_to_all(term, "seq", split_axis=0, concat_axis=0, tiled=True)
+    term = jnp.sum(term, axis=0)
+
+    def exchanged(weights):
+        return lax.all_to_all(
+            products(grads, weights, rows, block_rows), "dp", split_axis=0, concat_axis=0, tiled=True
+        )
+
+    def places(*distances):
+        return (seq_at.astype(jnp.int32) + jnp.array(distances, jnp.int32)) % seq_count
+
+    first = exchanged([held, before, after])
+    second = exchanged([two_before, two_after])
+    handed = placed_blocks(first, places(0, 4, 8, 12, 15, 3, 7, 11, 1, 5, 9, 13), seq_count)
+    handed = placed_blocks(second, places(14, 2, 6, 10), seq_count, handed)
     return (handed[None, None], term[None])
 
 

time: 154 us -> 142 us (0.922)
  the two profiles are of different devices: /device:TPU:12 before, /device:TPU:2 now
where the time goes in v2:
time: 142 us; the launch traced here: 141 us
  starting transfers between devices  80.7 us (57%)
  waiting for transfers between devices  32.8 us (23%)
  Pallas kernels  17.1 us (12%)
  local copies, waits for them, and re-layouts  5.78 us (4%)
  other arithmetic  2.19 us (2%)
    ppermute x16, starting transfers between devices, shifted(): return lax.ppermute(value, axes if len(axes) > 1 else axes[0], pairs)  59.6 us
    ppermute x16, waiting for transfers between devices, shifted(): return lax.ppermute(value, axes if len(axes) > 1 else axes[0], pairs)  15.5 us
    all_to_all x1, starting transfers between devices, local(): term = lax.all_to_all(term, 'seq', split_axis=0, concat_axis=0, tiled=True)  9.41 us
    all_to_all x2, waiting for transfers between devices, exchanged(): lax.all_to_all(products(grads, weights, rows, block_rows), 'dp', split_ax...  7.77 us
    all_to_all x2, starting transfers between devices, exchanged(): lax.all_to_all(products(grads, weights, rows, block_rows), 'dp', split_ax...  7.77 us
    all_to_all x1, waiting for transfers between devices, local(): term = lax.all_to_all(term, 'seq', split_axis=0, concat_axis=0, tiled=True)  7.58 us
    pallas_call x2, Pallas kernels, placed_blocks(): pl.pallas_call(placed_kernel, grid_spec=pltpu.PrefetchScalarGridSpec(num_...  6.77 us
    pallas_call x1, Pallas kernels, attention(): pl.pallas_call(functools.partial(attention_kernel, chunks=chunks, heads=g...  5.41 us
  transfers between devices with their start and end apart: 20, of which 10 were waited for; matrix products, arithmetic and copies ran while one was open for 3% of the time, Pallas kernels for 11%

profile of v2, /device:TPU:2, one launch (start us, length us, event | category | flops | bytes accessed | tf_op | source)
XLA Modules:
  0.0 140.6 jit_solution(283891696751013220)
XLA Ops:
  2.5 3.8 %collective-permute-start.2 = (bf16[144,512]{1,0:T(8,128)(2,1)S(1)}, bf16[144,512]{1,0:T(8,128)(2,1)S(1)}, u32[]{:S(2)}, u32[]{:S(2)}) collective-permute-start(bf16[144,512]{1,0:T(8,128)(2,1)S(1)} %shard_map.131.refs_3_), channel_id=1, source_target_pairs={{0,32},{32,64},{64,96},{96,128},{128,160},{160,192},{192,224},{224... | collective-permute-start | bytes 442376 | tf_op jit(solution)/shard_map/ppermute | solution.py:37
  6.3 5.2 %collective-permute-start.1 = (bf16[144,512]{1,0:T(8,128)(2,1)S(1)}, bf16[144,512]{1,0:T(8,128)(2,1)S(1)}, u32[]{:S(2)}, u32[]{:S(2)}) collective-permute-start(bf16[144,512]{1,0:T(8,128)(2,1)S(1)} %shard_map.131.refs_3_), channel_id=1, source_target_pairs={{0,64},{32,96},{64,128},{96,160},{128,192},{160,224},{192,256},{22... | collective-permute-start | bytes 442376 | tf_op jit(solution)/shard_map/ppermute | solution.py:37
  11.5 7.7 %collective-permute-start = (bf16[144,512]{1,0:T(8,128)(2,1)S(1)}, bf16[144,512]{1,0:T(8,128)(2,1)S(1)}, u32[]{:S(2)}, u32[]{:S(2)}) collective-permute-start(bf16[144,512]{1,0:T(8,128)(2,1)S(1)} %shard_map.131.refs_3_), channel_id=1, source_target_pairs={{0,96},{32,128},{64,160},{96,192},{128,224},{160,256},{192,288},{2... | collective-permute-start | bytes 442376 | tf_op jit(solution)/shard_map/ppermute | solution.py:37
  24.0 7.4 %collective-permute-start.8 = (bf16[128,512]{1,0:T(8,128)(2,1)S(1)}, bf16[128,512]{1,0:T(8,128)(2,1)S(1)}, u32[]{:S(2)}, u32[]{:S(2)}) collective-permute-start(bf16[128,512]{1,0:T(8,128)(2,1)S(1)} %fusion), channel_id=1, source_target_pairs={{4,128},{8,132},{12,136},{16,140},{20,144},{24,148},{28,152},{36,1... | collective-permute-start | bytes 393224 | tf_op jit(solution)/shard_map/ppermute | solution.py:37
  36.5 5.4 %shard_map.132 = (bf16[128,512]{1,0:T(8,128)(2,1)S(1)}, bf16[128,512]{1,0:T(8,128)(2,1)S(1)}, bf16[128,512]{1,0:T(8,128)(2,1)S(1)}, bf16[128,512]{1,0:T(8,128)(2,1)S(1)}) custom-call(bf16[128,4096]{1,0:T(8,128)(2,1)S(1)} %bitcast.23, bf16[128,4096]{1,0:T(8,128)(2,1)S(1)} %bitcast.24, f32[128,128]{1,0:T(8,128)S(1)} %broadcast_in_dim.12.w_ref, ...), custom_call_target="tpu_custom_call" | custom-call | flops 1073741824 | bytes 2097152 | tf_op jit(solution)/shard_map/pallas_call | solution.py:77
  49.1 8.3 %collective-permute-start.10 = (bf16[64,512]{1,0:T(8,128)(2,1)S(1)}, bf16[64,512]{1,0:T(8,128)(2,1)S(1)}, u32[]{:S(2)}, u32[]{:S(2)}) collective-permute-start(bf16[64,512]{1,0:T(8,128)(2,1)S(1)} %slice.16), channel_id=1, source_target_pairs={{0,128},{32,160},{64,192},{96,224},{128,256},{160,288},{192,320},{... | collective-permute-start | bytes 196616 | tf_op jit(solution)/shard_map/ppermute | solution.py:37
  57.4 2.3 %collective-permute-done.3.refs_0_ = bf16[128,512]{1,0:T(8,128)(2,1)S(1)} collective-permute-done((bf16[128,512]{1,0:T(8,128)(2,1)S(1)}, bf16[128,512]{1,0:T(8,128)(2,1)S(1)}, u32[]{:S(2)}, u32[]{:S(2)}) %collective-permute-start.3) | collective-permute-done | bytes 131104 | tf_op jit(solution)/shard_map/ppermute | solution.py:37
  59.7 5.9 %collective-permute-start.11 = (bf16[64,512]{1,0:T(8,128)(2,1)S(1)}, bf16[64,512]{1,0:T(8,128)(2,1)S(1)}, u32[]{:S(2)}, u32[]{:S(2)}) collective-permute-start(bf16[64,512]{1,0:T(8,128)(2,1)S(1)} %slice.17), channel_id=1, source_target_pairs={{0,384},{32,416},{64,448},{96,480},{128,0},{160,32},{192,64},{224,... | collective-permute-start | bytes 196616 | tf_op jit(solution)/shard_map/ppermute | solution.py:37
  66.9 3.9 %all-to-all-start = ((bf16[4,144,512]{2,1,0:T(8,128)(2,1)}), bf16[4,144,512]{2,1,0:T(8,128)(2,1)S(1)}, u32[]{:S(2)}, u32[]{:S(2)}) async-start(bf16[4,144,512]{2,1,0:T(8,128)(2,1)} %shard_map.134), calls=%async_computation | async-start | bytes 1179648 | tf_op jit(solution)/shard_map/all_to_all | solution.py:327
  70.8 2.5 %collective-permute-done.11.refs_3_ = bf16[64,512]{1,0:T(8,128)(2,1)S(1)} collective-permute-done((bf16[64,512]{1,0:T(8,128)(2,1)S(1)}, bf16[64,512]{1,0:T(8,128)(2,1)S(1)}, u32[]{:S(2)}, u32[]{:S(2)}) %collective-permute-start.11) | collective-permute-done | bytes 65568 | tf_op jit(solution)/shard_map/ppermute | solution.py:37
  75.4 3.9 %collective-permute-start.12 = (bf16[512,512]{1,0:T(8,128)(2,1)S(1)}, bf16[512,512]{1,0:T(8,128)(2,1)S(1)}, u32[]{:S(2)}, u32[]{:S(2)}) collective-permute-start(bf16[512,512]{1,0:T(8,128)(2,1)S(1)} %shard_map.135.refs_0_), channel_id=1, source_target_pairs={{0,32},{32,64},{64,96},{96,128},{128,160},{160,192},{192,224},{224... | collective-permute-start | bytes 1572872 | tf_op jit(solution)/shard_map/ppermute | solution.py:37
  82.0 9.4 %all-to-all-start.3 = ((f32[16,1,512]{2,1,0:T(1,128)}), f32[16,1,512]{2,1,0:T(1,128)S(1)}, u32[]{:S(2)}, u32[]{:S(2)}) async-start(f32[16,1,512]{2,1,0:T(1,128)} %copy.19), calls=%async_computation.3 | async-start | bytes 65536 | tf_op jit(solution)/shard_map/all_to_all | solution.py:330
  91.4 2.8 %collective-permute-done.12.refs_1_ = bf16[512,512]{1,0:T(8,128)(2,1)S(1)} collective-permute-done((bf16[512,512]{1,0:T(8,128)(2,1)S(1)}, bf16[512,512]{1,0:T(8,128)(2,1)S(1)}, u32[]{:S(2)}, u32[]{:S(2)}) %collective-permute-start.12) | collective-permute-done | bytes 524320 | tf_op jit(solution)/shard_map/ppermute | solution.py:37
  94.2 2.2 %shard_map.137 = bf16[4,12,128,128]{3,2,1,0:T(8,128)(2,1)} custom-call(bf16[4,144,512]{2,1,0:T(8,128)(2,1)S(1)} %all-to-all-done.grads_ref, bf16[512,512]{1,0:T(8,128)(2,1)S(1)} %shard_map.135.refs_0_, bf16[512,512]{1,0:T(8,128)(2,1)S(1)} %collective-permute-done.12.refs_1_, bf16[512,512]{1,0:T(8,128)(2,1)S(1)} %collective-permute-done.14.refs_2_), custom_call_target="tpu_custom_call" | custom-call | tf_op jit(solution)/shard_map/pallas_call | solution.py:202
  96.3 7.6 %all-to-all-done.3 = f32[16,1,512]{2,1,0:T(1,128)S(1)} async-done(((f32[16,1,512]{2,1,0:T(1,128)}), f32[16,1,512]{2,1,0:T(1,128)S(1)}, u32[]{:S(2)}, u32[]{:S(2)}) %all-to-all-start.3) | async-done | bytes 32800 | tf_op jit(solution)/shard_map/all_to_all | solution.py:330
  103.9 4.3 %all-to-all-start.2 = ((bf16[4,12,128,128]{3,2,1,0:T(8,128)(2,1)}), bf16[4,12,128,128]{3,2,1,0:T(8,128)(2,1)S(1)}, u32[]{:S(2)}, u32[]{:S(2)}) async-start(bf16[4,12,128,128]{3,2,1,0:T(8,128)(2,1)} %shard_map.137), calls=%async_computation.2 | async-start | bytes 3145728 | tf_op jit(solution)/shard_map/all_to_all | solution.py:334
  108.2 2.9 %collective-permute-start.15 = (bf16[256,512]{1,0:T(8,128)(2,1)S(1)}, bf16[256,512]{1,0:T(8,128)(2,1)S(1)}, u32[]{:S(2)}, u32[]{:S(2)}) collective-permute-start(bf16[256,512]{1,0:T(8,128)(2,1)S(1)} %slice.21), channel_id=1, source_target_pairs={{0,480},{32,0},{64,32},{96,64},{128,96},{160,128},{192,160},{224,1... | collective-permute-start | bytes 786440 | tf_op jit(solution)/shard_map/ppermute | solution.py:37
  111.2 2.9 %collective-permute-start.13 = (bf16[256,512]{1,0:T(8,128)(2,1)S(1)}, bf16[256,512]{1,0:T(8,128)(2,1)S(1)}, u32[]{:S(2)}, u32[]{:S(2)}) collective-permute-start(bf16[256,512]{1,0:T(8,128)(2,1)S(1)} %slice.20), channel_id=1, source_target_pairs={{0,32},{32,64},{64,96},{96,128},{128,160},{160,192},{192,224},{224... | collective-permute-start | bytes 786440 | tf_op jit(solution)/shard_map/ppermute | solution.py:37
  114.1 2.4 %collective-permute-done.15.refs_1_ = bf16[256,512]{1,0:T(8,128)(2,1)S(1)} collective-permute-done((bf16[256,512]{1,0:T(8,128)(2,1)S(1)}, bf16[256,512]{1,0:T(8,128)(2,1)S(1)}, u32[]{:S(2)}, u32[]{:S(2)}) %collective-permute-start.15) | collective-permute-done | bytes 262176 | tf_op jit(solution)/shard_map/ppermute | solution.py:37
  116.5 4.1 %collective-permute-done.13.refs_0_ = bf16[256,512]{1,0:T(8,128)(2,1)S(1)} collective-permute-done((bf16[256,512]{1,0:T(8,128)(2,1)S(1)}, bf16[256,512]{1,0:T(8,128)(2,1)S(1)}, u32[]{:S(2)}, u32[]{:S(2)}) %collective-permute-start.13) | collective-permute-done | bytes 262176 | tf_op jit(solution)/shard_map/ppermute | solution.py:37
  121.9 5.2 %all-to-all-done.2.in_ref = bf16[4,12,128,128]{3,2,1,0:T(8,128)(2,1)S(1)} async-done(((bf16[4,12,128,128]{3,2,1,0:T(8,128)(2,1)}), bf16[4,12,128,128]{3,2,1,0:T(8,128)(2,1)S(1)}, u32[]{:S(2)}, u32[]{:S(2)}) %all-to-all-start.2) | async-done | bytes 1572896 | tf_op jit(solution)/shard_map/all_to_all | solution.py:334
  127.1 3.5 %all-to-all-start.1 = ((bf16[4,4,128,128]{3,2,1,0:T(8,128)(2,1)}), bf16[4,4,128,128]{3,2,1,0:T(8,128)(2,1)S(1)}, u32[]{:S(2)}, u32[]{:S(2)}) async-start(bf16[4,4,128,128]{3,2,1,0:T(8,128)(2,1)} %shard_map.136), calls=%async_computation.1 | async-start | bytes 1048576 | tf_op jit(solution)/shard_map/all_to_all | solution.py:334
  131.2 4.8 %shard_map.138.refs_0_ = bf16[128,8192]{1,0:T(8,128)(2,1)} custom-call(s32[12]{0:T(128)S(1)} %and_select_fusion.places_ref, bf16[4,12,128,128]{3,2,1,0:T(8,128)(2,1)S(1)} %all-to-all-done.2.in_ref), custom_call_target="tpu_custom_call" | custom-call | tf_op jit(solution)/shard_map/pallas_call | solution.py:219
  136.0 2.6 %all-to-all-done.1.in_ref = bf16[4,4,128,128]{3,2,1,0:T(8,128)(2,1)S(1)} async-done(((bf16[4,4,128,128]{3,2,1,0:T(8,128)(2,1)}), bf16[4,4,128,128]{3,2,1,0:T(8,128)(2,1)S(1)}, u32[]{:S(2)}, u32[]{:S(2)}) %all-to-all-start.1) | async-done | bytes 524320 | tf_op jit(solution)/shard_map/all_to_all | solution.py:334
  (55 shorter events, 28.7 us)
Async XLA Ops:
  0.6 19.4 %copy-start = (bf16[1,64,512]{2,1,0:T(8,128)(2,1)S(1)}, bf16[1,64,512]{2,1,0:T(8,128)(2,1)}, u32[]{:S(2)}) copy-start(bf16[1,64,512]{2,1,0:T(8,128)(2,1)} %param.20) | copy-start | bytes 196612
  2.5 19.6 %collective-permute-start.2 = (bf16[144,512]{1,0:T(8,128)(2,1)S(1)}, bf16[144,512]{1,0:T(8,128)(2,1)S(1)}, u32[]{:S(2)}, u32[]{:S(2)}) collective-permute-start(bf16[144,512]{1,0:T(8,128)(2,1)S(1)} %shard_map.131.refs_3_), channel_id=1, source_target_pairs={{0,32},{32,64},{64,96},{96,128},{128,160},{160,192},{192,224},{224... | collective-permute-start | bytes 442376 | tf_op jit(solution)/shard_map/ppermute | solution.py:37
  6.3 27.7 %collective-permute-start.1 = (bf16[144,512]{1,0:T(8,128)(2,1)S(1)}, bf16[144,512]{1,0:T(8,128)(2,1)S(1)}, u32[]{:S(2)}, u32[]{:S(2)}) collective-permute-start(bf16[144,512]{1,0:T(8,128)(2,1)S(1)} %shard_map.131.refs_3_), channel_id=1, source_target_pairs={{0,64},{32,96},{64,128},{96,160},{128,192},{160,224},{192,256},{22... | collective-permute-start | bytes 442376 | tf_op jit(solution)/shard_map/ppermute | solution.py:37
  11.5 22.5 %collective-permute-start = (bf16[144,512]{1,0:T(8,128)(2,1)S(1)}, bf16[144,512]{1,0:T(8,128)(2,1)S(1)}, u32[]{:S(2)}, u32[]{:S(2)}) collective-permute-start(bf16[144,512]{1,0:T(8,128)(2,1)S(1)} %shard_map.131.refs_3_), channel_id=1, source_target_pairs={{0,96},{32,128},{64,160},{96,192},{128,224},{160,256},{192,288},{2... | collective-permute-start | bytes 442376 | tf_op jit(solution)/shard_map/ppermute | solution.py:37
  22.1 22.5 %collective-permute-start.9 = (bf16[128,512]{1,0:T(8,128)(2,1)S(1)}, bf16[128,512]{1,0:T(8,128)(2,1)S(1)}, u32[]{:S(2)}, u32[]{:S(2)}) collective-permute-start(bf16[128,512]{1,0:T(8,128)(2,1)S(1)} %fusion), channel_id=1, source_target_pairs={{4,0},{8,4},{12,8},{16,12},{20,16},{24,20},{28,24},{5,1},{9,5},{13... | collective-permute-start | bytes 393224 | tf_op jit(solution)/shard_map/ppermute | solution.py:37
  24.0 21.8 %collective-permute-start.8 = (bf16[128,512]{1,0:T(8,128)(2,1)S(1)}, bf16[128,512]{1,0:T(8,128)(2,1)S(1)}, u32[]{:S(2)}, u32[]{:S(2)}) collective-permute-start(bf16[128,512]{1,0:T(8,128)(2,1)S(1)} %fusion), channel_id=1, source_target_pairs={{4,128},{8,132},{12,136},{16,140},{20,144},{24,148},{28,152},{36,1... | collective-permute-start | bytes 393224 | tf_op jit(solution)/shard_map/ppermute | solution.py:37
  32.1 17.0 %collective-permute-start.7 = (bf16[128,512]{1,0:T(8,128)(2,1)S(1)}, bf16[128,512]{1,0:T(8,128)(2,1)S(1)}, u32[]{:S(2)}, u32[]{:S(2)}) collective-permute-start(bf16[128,512]{1,0:T(8,128)(2,1)S(1)} %fusion), channel_id=1, source_target_pairs={{4,384},{8,388},{12,392},{16,396},{20,400},{24,404},{28,408},{36,4... | collective-permute-start | bytes 393224 | tf_op jit(solution)/shard_map/ppermute | solution.py:37
  34.1 1.2 copy-start.2
  41.9 17.7 %collective-permute-start.3 = (bf16[128,512]{1,0:T(8,128)(2,1)S(1)}, bf16[128,512]{1,0:T(8,128)(2,1)S(1)}, u32[]{:S(2)}, u32[]{:S(2)}) collective-permute-start(bf16[128,512]{1,0:T(8,128)(2,1)S(1)} %get-tuple-element.12.refs_4_), channel_id=1, source_target_pairs={{100,0},{104,4},{108,8},{112,12},{116,16},{120,20},{124,24},{132,3... | collective-permute-start | bytes 393224 | tf_op jit(solution)/shard_map/ppermute | solution.py:37
  43.2 22.8 %collective-permute-start.4 = (bf16[128,512]{1,0:T(8,128)(2,1)S(1)}, bf16[128,512]{1,0:T(8,128)(2,1)S(1)}, u32[]{:S(2)}, u32[]{:S(2)}) collective-permute-start(bf16[128,512]{1,0:T(8,128)(2,1)S(1)} %get-tuple-element.13.refs_5_), channel_id=1, source_target_pairs={{68,0},{72,4},{76,8},{80,12},{84,16},{88,20},{92,24},{100,32},{104... | collective-permute-start | bytes 393224 | tf_op jit(solution)/shard_map/ppermute | solution.py:37
  44.6 21.5 %collective-permute-start.5 = (bf16[128,512]{1,0:T(8,128)(2,1)S(1)}, bf16[128,512]{1,0:T(8,128)(2,1)S(1)}, u32[]{:S(2)}, u32[]{:S(2)}) collective-permute-start(bf16[128,512]{1,0:T(8,128)(2,1)S(1)} %get-tuple-element.14.refs_6_), channel_id=1, source_target_pairs={{36,0},{40,4},{44,8},{48,12},{52,16},{56,20},{60,24},{68,32},{72,3... | collective-permute-start | bytes 393224 | tf_op jit(solution)/shard_map/ppermute | solution.py:37
  45.9 20.2 %collective-permute-start.6 = (bf16[128,512]{1,0:T(8,128)(2,1)S(1)}, bf16[128,512]{1,0:T(8,128)(2,1)S(1)}, u32[]{:S(2)}, u32[]{:S(2)}) collective-permute-start(bf16[128,512]{1,0:T(8,128)(2,1)S(1)} %get-tuple-element.15.refs_7_), channel_id=1, source_target_pairs={{4,0},{8,4},{12,8},{16,12},{20,16},{24,20},{28,24},{5,1},{9,5},{13... | collective-permute-start | bytes 393224 | tf_op jit(solution)/shard_map/ppermute | solution.py:37
  49.1 21.7 %collective-permute-start.10 = (bf16[64,512]{1,0:T(8,128)(2,1)S(1)}, bf16[64,512]{1,0:T(8,128)(2,1)S(1)}, u32[]{:S(2)}, u32[]{:S(2)}) collective-permute-start(bf16[64,512]{1,0:T(8,128)(2,1)S(1)} %slice.16), channel_id=1, source_target_pairs={{0,128},{32,160},{64,192},{96,224},{128,256},{160,288},{192,320},{... | collective-permute-start | bytes 196616 | tf_op jit(solution)/shard_map/ppermute | solution.py:37
  59.7 13.7 %collective-permute-start.11 = (bf16[64,512]{1,0:T(8,128)(2,1)S(1)}, bf16[64,512]{1,0:T(8,128)(2,1)S(1)}, u32[]{:S(2)}, u32[]{:S(2)}) collective-permute-start(bf16[64,512]{1,0:T(8,128)(2,1)S(1)} %slice.17), channel_id=1, source_target_pairs={{0,384},{32,416},{64,448},{96,480},{128,0},{160,32},{192,64},{224,... | collective-permute-start | bytes 196616 | tf_op jit(solution)/shard_map/ppermute | solution.py:37
  66.9 14.4 %all-to-all-start = ((bf16[4,144,512]{2,1,0:T(8,128)(2,1)}), bf16[4,144,512]{2,1,0:T(8,128)(2,1)S(1)}, u32[]{:S(2)}, u32[]{:S(2)}) async-start(bf16[4,144,512]{2,1,0:T(8,128)(2,1)} %shard_map.134), calls=%async_computation | async-start | bytes 1179648 | tf_op jit(solution)/shard_map/all_to_all | solution.py:327
  73.4 18.0 %collective-permute-start.14 = (bf16[512,512]{1,0:T(8,128)(2,1)S(1)}, bf16[512,512]{1,0:T(8,128)(2,1)S(1)}, u32[]{:S(2)}, u32[]{:S(2)}) collective-permute-start(bf16[512,512]{1,0:T(8,128)(2,1)S(1)} %shard_map.135.refs_0_), channel_id=1, source_target_pairs={{0,480},{32,0},{64,32},{96,64},{128,96},{160,128},{192,160},{224,1... | collective-permute-start | bytes 1572872 | tf_op jit(solution)/shard_map/ppermute | solution.py:37
  75.4 18.8 %collective-permute-start.12 = (bf16[512,512]{1,0:T(8,128)(2,1)S(1)}, bf16[512,512]{1,0:T(8,128)(2,1)S(1)}, u32[]{:S(2)}, u32[]{:S(2)}) collective-permute-start(bf16[512,512]{1,0:T(8,128)(2,1)S(1)} %shard_map.135.refs_0_), channel_id=1, source_target_pairs={{0,32},{32,64},{64,96},{96,128},{128,160},{160,192},{192,224},{224... | collective-permute-start | bytes 1572872 | tf_op jit(solution)/shard_map/ppermute | solution.py:37
  82.0 22.0 %all-to-all-start.3 = ((f32[16,1,512]{2,1,0:T(1,128)}), f32[16,1,512]{2,1,0:T(1,128)S(1)}, u32[]{:S(2)}, u32[]{:S(2)}) async-start(f32[16,1,512]{2,1,0:T(1,128)} %copy.19), calls=%async_computation.3 | async-start | bytes 65536 | tf_op jit(solution)/shard_map/all_to_all | solution.py:330
  103.9 23.2 %all-to-all-start.2 = ((bf16[4,12,128,128]{3,2,1,0:T(8,128)(2,1)}), bf16[4,12,128,128]{3,2,1,0:T(8,128)(2,1)S(1)}, u32[]{:S(2)}, u32[]{:S(2)}) async-start(bf16[4,12,128,128]{3,2,1,0:T(8,128)(2,1)} %shard_map.137), calls=%async_computation.2 | async-start | bytes 3145728 | tf_op jit(solution)/shard_map/all_to_all | solution.py:334
  108.2 22.3 %copy-start.5 = (s32[12]{0:T(128)S(1)}, s32[12]{0:T(128)}, u32[]{:S(2)}) copy-start(s32[12]{0:T(128)} %constant.50.clone) | copy-start | bytes 148
  108.2 22.4 %copy-start.4 = (s32[4]{0:T(128)S(1)}, s32[4]{0:T(128)}, u32[]{:S(2)}) copy-start(s32[4]{0:T(128)} %constant.51.clone) | copy-start | bytes 52
  108.2 8.3 %collective-permute-start.15 = (bf16[256,512]{1,0:T(8,128)(2,1)S(1)}, bf16[256,512]{1,0:T(8,128)(2,1)S(1)}, u32[]{:S(2)}, u32[]{:S(2)}) collective-permute-start(bf16[256,512]{1,0:T(8,128)(2,1)S(1)} %slice.21), channel_id=1, source_target_pairs={{0,480},{32,0},{64,32},{96,64},{128,96},{160,128},{192,160},{224,1... | collective-permute-start | bytes 786440 | tf_op jit(solution)/shard_map/ppermute | solution.py:37
  111.2 9.5 %collective-permute-start.13 = (bf16[256,512]{1,0:T(8,128)(2,1)S(1)}, bf16[256,512]{1,0:T(8,128)(2,1)S(1)}, u32[]{:S(2)}, u32[]{:S(2)}) collective-permute-start(bf16[256,512]{1,0:T(8,128)(2,1)S(1)} %slice.20), channel_id=1, source_target_pairs={{0,32},{32,64},{64,96},{96,128},{128,160},{160,192},{192,224},{224... | collective-permute-start | bytes 786440 | tf_op jit(solution)/shard_map/ppermute | solution.py:37
  127.1 11.5 %all-to-all-start.1 = ((bf16[4,4,128,128]{3,2,1,0:T(8,128)(2,1)}), bf16[4,4,128,128]{3,2,1,0:T(8,128)(2,1)S(1)}, u32[]{:S(2)}, u32[]{:S(2)}) async-start(bf16[4,4,128,128]{3,2,1,0:T(8,128)(2,1)} %shard_map.136), calls=%async_computation.1 | async-start | bytes 1048576 | tf_op jit(solution)/shard_map/all_to_all | solution.py:334
  (2 other events, 2.1 us)

commit v3 on v2

--- a/solution.py
+++ b/solution.py
@@ -181,52 +181,90 @@
     )(*arrays)
 
 
-def product_kernel(grads_ref, *refs):
-    weight_refs, out_ref = refs[:-1], refs[-1]
+def product_kernel(grads_ref, *refs, weights):
+    weight_refs, out_refs = refs[:weights], refs[weights:]
     members, _, width = grads_ref.shape
-    _, _, rows, block_rows = out_ref.shape
+    rows, block_rows = out_refs[0].shape[-2:]
     grads = grads_ref[:, :rows].reshape(members * rows, width)
     block = 0
     for ref in weight_refs:
         values = lax.dot_general(
             grads, ref[...], (((1,), (1,)), ((), ())), preferred_element_type=jnp.float32
-        ).astype(out_ref.dtype)
+        ).astype(out_refs[0].dtype)
         for k in range(ref.shape[0] // block_rows):
             part = values[:, k * block_rows : (k + 1) * block_rows]
-            out_ref[:, block] = part.reshape(members, rows, block_rows)
+            out_refs[0][:, block] = part.reshape(members, rows, block_rows)
             block += 1
 
 
 def products(grads, weights, rows, block_rows):
     blocks = sum(weight.shape[0] for weight in weights) // block_rows
     return pl.pallas_call(
-        product_kernel,
+        functools.partial(product_kernel, weights=len(weights)),
         out_shape=jax.ShapeDtypeStruct((grads.shape[0], blocks, rows, block_rows), grads.dtype),
         compiler_params=pltpu.CompilerParams(vmem_limit_bytes=48 * 1024 * 1024),
     )(grads, *weights)
 
 
-def placed_kernel(places_ref, in_ref, *refs):
-    out_ref = refs[-1]
-    members, _, _, size = in_ref.shape
-    for member in range(members):
-        out_ref[:, member * size : (member + 1) * size] = in_ref[member, 0]
-
-
-def placed_blocks(exchanged, places, count, before=None):
-    members, blocks, rows, size = exchanged.shape
+def placed_kernel(members_ref, places_ref, *refs, count):
+    part_refs, out_ref, sems = refs[:count], refs[-2], refs[-1]
+    blocks, _, size = part_refs[0].shape
+    copies = []
+    for block in range(blocks):
+        for index, ref in enumerate(part_refs):
+            at = pl.multiple_of((places_ref[block] * count + members_ref[index]) * size, size)
+            copy = pltpu.make_async_copy(
+                ref.at[block], out_ref.at[:, pl.ds(at, size)], sems.at[block, index]
+            )
+            copy.start()
+            copies.append(copy)
+    for copy in copies:
+        copy.wait()
+
+
+def placed_parts(parts, members, places, width, before=None):
+    blocks, rows, _ = parts[0].shape
+    anywhere = pl.BlockSpec(memory_space=pl.ANY)
+    scalar = pl.BlockSpec(memory_space=pltpu.SMEM)
+    operands = list(parts) + ([] if before is None else [before])
+    return pl.pallas_call(
+        functools.partial(placed_kernel, count=len(parts)),
+        in_specs=[scalar, scalar] + [anywhere] * len(operands),
+        out_specs=anywhere,
+        out_shape=jax.ShapeDtypeStruct((rows, width), parts[0].dtype),
+        input_output_aliases={} if before is None else {2 + len(parts): 0},
+        scratch_shapes=[pltpu.SemaphoreType.DMA((blocks, len(parts)))],
+        compiler_params=pltpu.CompilerParams(vmem_limit_bytes=32 * 1024 * 1024),
+    )(members, places, *operands)
+
+
+def placed_whole_kernel(places_ref, in_ref, *refs):
+    out_ref, sems = refs[-2], refs[-1]
+    members, blocks, _, size = in_ref.shape
+    copies = []
+    for block in range(blocks):
+        for member in range(members):
+            at = pl.multiple_of((places_ref[block] * members + member) * size, size)
+            copy = pltpu.make_async_copy(
+                in_ref.at[member, block], out_ref.at[:, pl.ds(at, size)], sems.at[block, member]
+            )
+            copy.start()
+            copies.append(copy)
+    for copy in copies:
+        copy.wait()
+
+
+def placed_whole(exchanged, places, width, before=None):
+    members, blocks, rows, _ = exchanged.shape
+    anywhere = pl.BlockSpec(memory_space=pl.ANY)
     operands = [exchanged] + ([] if before is None else [before])
     return pl.pallas_call(
-        placed_kernel,
-        grid_spec=pltpu.PrefetchScalarGridSpec(
-            num_scalar_prefetch=1,
-            grid=(blocks,),
-            in_specs=[pl.BlockSpec((members, 1, rows, size), lambda i, places: (0, i, 0, 0))]
-            + ([] if before is None else [pl.BlockSpec(memory_space=pl.ANY)]),
-            out_specs=pl.BlockSpec((rows, members * size), lambda i, places: (0, places[i])),
-        ),
-        out_shape=jax.ShapeDtypeStruct((rows, count * members * size), exchanged.dtype),
+        placed_whole_kernel,
+        in_specs=[pl.BlockSpec(memory_space=pltpu.SMEM)] + [anywhere] * len(operands),
+        out_specs=anywhere,
+        out_shape=jax.ShapeDtypeStruct((rows, width), exchanged.dtype),
         input_output_aliases={} if before is None else {2: 0},
+        scratch_shapes=[pltpu.SemaphoreType.DMA((blocks, members))],
         compiler_params=pltpu.CompilerParams(vmem_limit_bytes=32 * 1024 * 1024),
     )(places, *operands)
 
@@ -335,13 +373,27 @@
             products(grads, weights, rows, block_rows), "dp", split_axis=0, concat_axis=0, tiled=True
         )
 
+    def passed(weights):
+        product = products(grads, weights, rows, block_rows)
+        parts = []
+        for step in range(dp_count):
+            at = (dp_at + step) % dp_count
+            part = lax.dynamic_index_in_dim(product, at, 0, keepdims=False)
+            parts.append(shifted(part, {"dp": step}, cyclic=("dp",)) if step else part)
+        return parts
+
     def places(*distances):
         return (seq_at.astype(jnp.int32) + jnp.array(distances, jnp.int32)) % seq_count
 
+    dp_at = lax.axis_index("dp").astype(jnp.int32)
+    members = (dp_at - jnp.arange(dp_count, dtype=jnp.int32)) % dp_count
+    width = seq_count * dp_count * block_rows
+    first_places = places(0, 4, 8, 12, 15, 3, 7, 11, 1, 5, 9, 13)
+    second_places = places(14, 2, 6, 10)
     first = exchanged([held, before, after])
+    handed = placed_whole(first, first_places, width)
     second = exchanged([two_before, two_after])
-    handed = placed_blocks(first, places(0, 4, 8, 12, 15, 3, 7, 11, 1, 5, 9, 13), seq_count)
-    handed = placed_blocks(second, places(14, 2, 6, 10), seq_count, handed)
+    handed = placed_whole(second, second_places, width, handed)
     return (handed[None, None], term[None])
 
 

time: 142 us -> 141 us (level)
  Pallas kernels: 17.1 us -> 13.8 us
  waiting for transfers between devices: 32.8 us -> 35.5 us
    pallas_call x4, Pallas kernels: 10.2 us -> 6.98 us  [the longest x2 3.54 us: placed_whole(): pl.pallas_call(placed_whole_kernel, in_specs=[pl.BlockSpec(memory_space=p...]
    all_to_all x2, waiting for transfers between devices: 7.77 us -> 10.4 us  [exchanged(): lax.all_to_all(products(grads, weights, rows, block_rows), 'dp', split_ax...]
  transfers between devices with their start and end apart: 20 -> 20, of which waited for: 10 -> 10; matrix products, arithmetic and copies ran while one was open for 3% -> 3% of each run, Pallas kernels for 11% -> 9%
where the time goes in v3:
time: 141 us; the launch traced here: 140 us
  starting transfers between devices  80.7 us (57%)
  waiting for transfers between devices  35.5 us (25%)
  Pallas kernels  13.8 us (10%)
  local copies, waits for them, and re-layouts  5.78 us (4%)
  other arithmetic  2.19 us (2%)
    ppermute x16, starting transfers between devices, shifted(): return lax.ppermute(value, axes if len(axes) > 1 else axes[0], pairs)  59.6 us
    ppermute x16, waiting for transfers between devices, shifted(): return lax.ppermute(value, axes if len(axes) > 1 else axes[0], pairs)  15.5 us
    all_to_all x2, waiting for transfers between devices, exchanged(): lax.all_to_all(products(grads, weights, rows, block_rows), 'dp', split_ax...  10.4 us
    all_to_all x1, starting transfers between devices, local(): term = lax.all_to_all(term, 'seq', split_axis=0, concat_axis=0, tiled=True)  9.41 us
    all_to_all x2, starting transfers between devices, exchanged(): lax.all_to_all(products(grads, weights, rows, block_rows), 'dp', split_ax...  7.77 us
    all_to_all x1, waiting for transfers between devices, local(): term = lax.all_to_all(term, 'seq', split_axis=0, concat_axis=0, tiled=True)  7.58 us
    pallas_call x1, Pallas kernels, attention(): pl.pallas_call(functools.partial(attention_kernel, chunks=chunks, heads=g...  5.41 us
    unnamed x13, local copies, waits for them, and re-layouts  4.23 us
  transfers between devices with their start and end apart: 20, of which 10 were waited for; matrix products, arithmetic and copies ran while one was open for 3% of the time, Pallas kernels for 9%

profile of v3, /device:TPU:2, one launch (start us, length us, event | category | flops | bytes accessed | tf_op | source)
XLA Modules:
  0.0 140.1 jit_solution(12535611817693114995)
XLA Ops:
  2.5 3.8 %collective-permute-start.2 = (bf16[144,512]{1,0:T(8,128)(2,1)S(1)}, bf16[144,512]{1,0:T(8,128)(2,1)S(1)}, u32[]{:S(2)}, u32[]{:S(2)}) collective-permute-start(bf16[144,512]{1,0:T(8,128)(2,1)S(1)} %shard_map.131.refs_3_), channel_id=1, source_target_pairs={{0,32},{32,64},{64,96},{96,128},{128,160},{160,192},{192,224},{224... | collective-permute-start | bytes 442376 | tf_op jit(solution)/shard_map/ppermute | solution.py:37
  6.3 5.2 %collective-permute-start.1 = (bf16[144,512]{1,0:T(8,128)(2,1)S(1)}, bf16[144,512]{1,0:T(8,128)(2,1)S(1)}, u32[]{:S(2)}, u32[]{:S(2)}) collective-permute-start(bf16[144,512]{1,0:T(8,128)(2,1)S(1)} %shard_map.131.refs_3_), channel_id=1, source_target_pairs={{0,64},{32,96},{64,128},{96,160},{128,192},{160,224},{192,256},{22... | collective-permute-start | bytes 442376 | tf_op jit(solution)/shard_map/ppermute | solution.py:37
  11.5 7.7 %collective-permute-start = (bf16[144,512]{1,0:T(8,128)(2,1)S(1)}, bf16[144,512]{1,0:T(8,128)(2,1)S(1)}, u32[]{:S(2)}, u32[]{:S(2)}) collective-permute-start(bf16[144,512]{1,0:T(8,128)(2,1)S(1)} %shard_map.131.refs_3_), channel_id=1, source_target_pairs={{0,96},{32,128},{64,160},{96,192},{128,224},{160,256},{192,288},{2... | collective-permute-start | bytes 442376 | tf_op jit(solution)/shard_map/ppermute | solution.py:37
  24.0 7.4 %collective-permute-start.8 = (bf16[128,512]{1,0:T(8,128)(2,1)S(1)}, bf16[128,512]{1,0:T(8,128)(2,1)S(1)}, u32[]{:S(2)}, u32[]{:S(2)}) collective-permute-start(bf16[128,512]{1,0:T(8,128)(2,1)S(1)} %fusion), channel_id=1, source_target_pairs={{4,128},{8,132},{12,136},{16,140},{20,144},{24,148},{28,152},{36,1... | collective-permute-start | bytes 393224 | tf_op jit(solution)/shard_map/ppermute | solution.py:37
  36.5 5.4 %shard_map.132 = (bf16[128,512]{1,0:T(8,128)(2,1)S(1)}, bf16[128,512]{1,0:T(8,128)(2,1)S(1)}, bf16[128,512]{1,0:T(8,128)(2,1)S(1)}, bf16[128,512]{1,0:T(8,128)(2,1)S(1)}) custom-call(bf16[128,4096]{1,0:T(8,128)(2,1)S(1)} %bitcast.23, bf16[128,4096]{1,0:T(8,128)(2,1)S(1)} %bitcast.24, f32[128,128]{1,0:T(8,128)S(1)} %broadcast_in_dim.12.w_ref, ...), custom_call_target="tpu_custom_call" | custom-call | flops 1073741824 | bytes 2097152 | tf_op jit(solution)/shard_map/pallas_call | solution.py:77
  49.1 8.3 %collective-permute-start.10 = (bf16[64,512]{1,0:T(8,128)(2,1)S(1)}, bf16[64,512]{1,0:T(8,128)(2,1)S(1)}, u32[]{:S(2)}, u32[]{:S(2)}) collective-permute-start(bf16[64,512]{1,0:T(8,128)(2,1)S(1)} %slice.16), channel_id=1, source_target_pairs={{0,128},{32,160},{64,192},{96,224},{128,256},{160,288},{192,320},{... | collective-permute-start | bytes 196616 | tf_op jit(solution)/shard_map/ppermute | solution.py:37
  57.4 2.3 %collective-permute-done.3.refs_0_ = bf16[128,512]{1,0:T(8,128)(2,1)S(1)} collective-permute-done((bf16[128,512]{1,0:T(8,128)(2,1)S(1)}, bf16[128,512]{1,0:T(8,128)(2,1)S(1)}, u32[]{:S(2)}, u32[]{:S(2)}) %collective-permute-start.3) | collective-permute-done | bytes 131104 | tf_op jit(solution)/shard_map/ppermute | solution.py:37
  59.7 5.9 %collective-permute-start.11 = (bf16[64,512]{1,0:T(8,128)(2,1)S(1)}, bf16[64,512]{1,0:T(8,128)(2,1)S(1)}, u32[]{:S(2)}, u32[]{:S(2)}) collective-permute-start(bf16[64,512]{1,0:T(8,128)(2,1)S(1)} %slice.17), channel_id=1, source_target_pairs={{0,384},{32,416},{64,448},{96,480},{128,0},{160,32},{192,64},{224,... | collective-permute-start | bytes 196616 | tf_op jit(solution)/shard_map/ppermute | solution.py:37
  66.9 3.9 %all-to-all-start = ((bf16[4,144,512]{2,1,0:T(8,128)(2,1)}), bf16[4,144,512]{2,1,0:T(8,128)(2,1)S(1)}, u32[]{:S(2)}, u32[]{:S(2)}) async-start(bf16[4,144,512]{2,1,0:T(8,128)(2,1)} %shard_map.134), calls=%async_computation | async-start | bytes 1179648 | tf_op jit(solution)/shard_map/all_to_all | solution.py:365
  70.8 2.5 %collective-permute-done.11.refs_3_ = bf16[64,512]{1,0:T(8,128)(2,1)S(1)} collective-permute-done((bf16[64,512]{1,0:T(8,128)(2,1)S(1)}, bf16[64,512]{1,0:T(8,128)(2,1)S(1)}, u32[]{:S(2)}, u32[]{:S(2)}) %collective-permute-start.11) | collective-permute-done | bytes 65568 | tf_op jit(solution)/shard_map/ppermute | solution.py:37
  75.4 3.9 %collective-permute-start.12 = (bf16[512,512]{1,0:T(8,128)(2,1)S(1)}, bf16[512,512]{1,0:T(8,128)(2,1)S(1)}, u32[]{:S(2)}, u32[]{:S(2)}) collective-permute-start(bf16[512,512]{1,0:T(8,128)(2,1)S(1)} %shard_map.135.refs_0_), channel_id=1, source_target_pairs={{0,32},{32,64},{64,96},{96,128},{128,160},{160,192},{192,224},{224... | collective-permute-start | bytes 1572872 | tf_op jit(solution)/shard_map/ppermute | solution.py:37
  82.0 9.4 %all-to-all-start.3 = ((f32[16,1,512]{2,1,0:T(1,128)}), f32[16,1,512]{2,1,0:T(1,128)S(1)}, u32[]{:S(2)}, u32[]{:S(2)}) async-start(f32[16,1,512]{2,1,0:T(1,128)} %copy.19), calls=%async_computation.3 | async-start | bytes 65536 | tf_op jit(solution)/shard_map/all_to_all | solution.py:368
  91.4 2.8 %collective-permute-done.12.refs_1_ = bf16[512,512]{1,0:T(8,128)(2,1)S(1)} collective-permute-done((bf16[512,512]{1,0:T(8,128)(2,1)S(1)}, bf16[512,512]{1,0:T(8,128)(2,1)S(1)}, u32[]{:S(2)}, u32[]{:S(2)}) %collective-permute-start.12) | collective-permute-done | bytes 524320 | tf_op jit(solution)/shard_map/ppermute | solution.py:37
  94.2 2.2 %shard_map.137 = bf16[4,12,128,128]{3,2,1,0:T(8,128)(2,1)} custom-call(bf16[4,144,512]{2,1,0:T(8,128)(2,1)S(1)} %all-to-all-done.grads_ref, bf16[512,512]{1,0:T(8,128)(2,1)S(1)} %shard_map.135.refs_0_, bf16[512,512]{1,0:T(8,128)(2,1)S(1)} %collective-permute-done.12.refs_1_, bf16[512,512]{1,0:T(8,128)(2,1)S(1)} %collective-permute-done.14.refs_2_), custom_call_target="tpu_custom_call" | custom-call | tf_op jit(solution)/shard_map/pallas_call | solution.py:202
  96.3 7.6 %all-to-all-done.3 = f32[16,1,512]{2,1,0:T(1,128)S(1)} async-done(((f32[16,1,512]{2,1,0:T(1,128)}), f32[16,1,512]{2,1,0:T(1,128)S(1)}, u32[]{:S(2)}, u32[]{:S(2)}) %all-to-all-start.3) | async-done | bytes 32800 | tf_op jit(solution)/shard_map/all_to_all | solution.py:368
  103.9 4.3 %all-to-all-start.2 = ((bf16[4,12,128,128]{3,2,1,0:T(8,128)(2,1)}), bf16[4,12,128,128]{3,2,1,0:T(8,128)(2,1)S(1)}, u32[]{:S(2)}, u32[]{:S(2)}) async-start(bf16[4,12,128,128]{3,2,1,0:T(8,128)(2,1)} %shard_map.137), calls=%async_computation.2 | async-start | bytes 3145728 | tf_op jit(solution)/shard_map/all_to_all | solution.py:372
  108.2 2.9 %collective-permute-start.15 = (bf16[256,512]{1,0:T(8,128)(2,1)S(1)}, bf16[256,512]{1,0:T(8,128)(2,1)S(1)}, u32[]{:S(2)}, u32[]{:S(2)}) collective-permute-start(bf16[256,512]{1,0:T(8,128)(2,1)S(1)} %slice.21), channel_id=1, source_target_pairs={{0,480},{32,0},{64,32},{96,64},{128,96},{160,128},{192,160},{224,1... | collective-permute-start | bytes 786440 | tf_op jit(solution)/shard_map/ppermute | solution.py:37
  111.2 2.9 %collective-permute-start.13 = (bf16[256,512]{1,0:T(8,128)(2,1)S(1)}, bf16[256,512]{1,0:T(8,128)(2,1)S(1)}, u32[]{:S(2)}, u32[]{:S(2)}) collective-permute-start(bf16[256,512]{1,0:T(8,128)(2,1)S(1)} %slice.20), channel_id=1, source_target_pairs={{0,32},{32,64},{64,96},{96,128},{128,160},{160,192},{192,224},{224... | collective-permute-start | bytes 786440 | tf_op jit(solution)/shard_map/ppermute | solution.py:37
  114.1 2.4 %collective-permute-done.15.refs_1_ = bf16[256,512]{1,0:T(8,128)(2,1)S(1)} collective-permute-done((bf16[256,512]{1,0:T(8,128)(2,1)S(1)}, bf16[256,512]{1,0:T(8,128)(2,1)S(1)}, u32[]{:S(2)}, u32[]{:S(2)}) %collective-permute-start.15) | collective-permute-done | bytes 262176 | tf_op jit(solution)/shard_map/ppermute | solution.py:37
  116.5 4.1 %collective-permute-done.13.refs_0_ = bf16[256,512]{1,0:T(8,128)(2,1)S(1)} collective-permute-done((bf16[256,512]{1,0:T(8,128)(2,1)S(1)}, bf16[256,512]{1,0:T(8,128)(2,1)S(1)}, u32[]{:S(2)}, u32[]{:S(2)}) %collective-permute-start.13) | collective-permute-done | bytes 262176 | tf_op jit(solution)/shard_map/ppermute | solution.py:37
  121.9 5.2 %all-to-all-done.2.in_ref = bf16[4,12,128,128]{3,2,1,0:T(8,128)(2,1)S(1)} async-done(((bf16[4,12,128,128]{3,2,1,0:T(8,128)(2,1)}), bf16[4,12,128,128]{3,2,1,0:T(8,128)(2,1)S(1)}, u32[]{:S(2)}, u32[]{:S(2)}) %all-to-all-start.2) | async-done | bytes 1572896 | tf_op jit(solution)/shard_map/all_to_all | solution.py:372
  127.1 3.5 %all-to-all-start.1 = ((bf16[4,4,128,128]{3,2,1,0:T(8,128)(2,1)}), bf16[4,4,128,128]{3,2,1,0:T(8,128)(2,1)S(1)}, u32[]{:S(2)}, u32[]{:S(2)}) async-start(bf16[4,4,128,128]{3,2,1,0:T(8,128)(2,1)} %shard_map.136), calls=%async_computation.1 | async-start | bytes 1048576 | tf_op jit(solution)/shard_map/all_to_all | solution.py:372
  131.2 2.1 %shard_map.138.refs_0_ = bf16[128,8192]{1,0:T(8,128)(2,1)} custom-call(s32[12]{0:T(128)S(1)} %and_select_fusion.places_ref, bf16[4,12,128,128]{3,2,1,0:T(8,128)(2,1)S(1)} %all-to-all-done.2.in_ref), custom_call_target="tpu_custom_call" | custom-call | tf_op jit(solution)/shard_map/pallas_call | solution.py:261
  133.3 5.3 %all-to-all-done.1.in_ref = bf16[4,4,128,128]{3,2,1,0:T(8,128)(2,1)S(1)} async-done(((bf16[4,4,128,128]{3,2,1,0:T(8,128)(2,1)}), bf16[4,4,128,128]{3,2,1,0:T(8,128)(2,1)S(1)}, u32[]{:S(2)}, u32[]{:S(2)}) %all-to-all-start.1) | async-done | bytes 524320 | tf_op jit(solution)/shard_map/all_to_all | solution.py:372
  (55 shorter events, 28.2 us)
Async XLA Ops:
  0.6 19.4 %copy-start = (bf16[1,64,512]{2,1,0:T(8,128)(2,1)S(1)}, bf16[1,64,512]{2,1,0:T(8,128)(2,1)}, u32[]{:S(2)}) copy-start(bf16[1,64,512]{2,1,0:T(8,128)(2,1)} %param.20) | copy-start | bytes 196612
  2.5 19.6 %collective-permute-start.2 = (bf16[144,512]{1,0:T(8,128)(2,1)S(1)}, bf16[144,512]{1,0:T(8,128)(2,1)S(1)}, u32[]{:S(2)}, u32[]{:S(2)}) collective-permute-start(bf16[144,512]{1,0:T(8,128)(2,1)S(1)} %shard_map.131.refs_3_), channel_id=1, source_target_pairs={{0,32},{32,64},{64,96},{96,128},{128,160},{160,192},{192,224},{224... | collective-permute-start | bytes 442376 | tf_op jit(solution)/shard_map/ppermute | solution.py:37
  6.3 27.7 %collective-permute-start.1 = (bf16[144,512]{1,0:T(8,128)(2,1)S(1)}, bf16[144,512]{1,0:T(8,128)(2,1)S(1)}, u32[]{:S(2)}, u32[]{:S(2)}) collective-permute-start(bf16[144,512]{1,0:T(8,128)(2,1)S(1)} %shard_map.131.refs_3_), channel_id=1, source_target_pairs={{0,64},{32,96},{64,128},{96,160},{128,192},{160,224},{192,256},{22... | collective-permute-start | bytes 442376 | tf_op jit(solution)/shard_map/ppermute | solution.py:37
  11.5 22.5 %collective-permute-start = (bf16[144,512]{1,0:T(8,128)(2,1)S(1)}, bf16[144,512]{1,0:T(8,128)(2,1)S(1)}, u32[]{:S(2)}, u32[]{:S(2)}) collective-permute-start(bf16[144,512]{1,0:T(8,128)(2,1)S(1)} %shard_map.131.refs_3_), channel_id=1, source_target_pairs={{0,96},{32,128},{64,160},{96,192},{128,224},{160,256},{192,288},{2... | collective-permute-start | bytes 442376 | tf_op jit(solution)/shard_map/ppermute | solution.py:37
  22.1 22.5 %collective-permute-start.9 = (bf16[128,512]{1,0:T(8,128)(2,1)S(1)}, bf16[128,512]{1,0:T(8,128)(2,1)S(1)}, u32[]{:S(2)}, u32[]{:S(2)}) collective-permute-start(bf16[128,512]{1,0:T(8,128)(2,1)S(1)} %fusion), channel_id=1, source_target_pairs={{4,0},{8,4},{12,8},{16,12},{20,16},{24,20},{28,24},{5,1},{9,5},{13... | collective-permute-start | bytes 393224 | tf_op jit(solution)/shard_map/ppermute | solution.py:37
  24.0 21.8 %collective-permute-start.8 = (bf16[128,512]{1,0:T(8,128)(2,1)S(1)}, bf16[128,512]{1,0:T(8,128)(2,1)S(1)}, u32[]{:S(2)}, u32[]{:S(2)}) collective-permute-start(bf16[128,512]{1,0:T(8,128)(2,1)S(1)} %fusion), channel_id=1, source_target_pairs={{4,128},{8,132},{12,136},{16,140},{20,144},{24,148},{28,152},{36,1... | collective-permute-start | bytes 393224 | tf_op jit(solution)/shard_map/ppermute | solution.py:37
  32.1 17.0 %collective-permute-start.7 = (bf16[128,512]{1,0:T(8,128)(2,1)S(1)}, bf16[128,512]{1,0:T(8,128)(2,1)S(1)}, u32[]{:S(2)}, u32[]{:S(2)}) collective-permute-start(bf16[128,512]{1,0:T(8,128)(2,1)S(1)} %fusion), channel_id=1, source_target_pairs={{4,384},{8,388},{12,392},{16,396},{20,400},{24,404},{28,408},{36,4... | collective-permute-start | bytes 393224 | tf_op jit(solution)/shard_map/ppermute | solution.py:37
  34.1 1.2 copy-start.2
  41.9 17.7 %collective-permute-start.3 = (bf16[128,512]{1,0:T(8,128)(2,1)S(1)}, bf16[128,512]{1,0:T(8,128)(2,1)S(1)}, u32[]{:S(2)}, u32[]{:S(2)}) collective-permute-start(bf16[128,512]{1,0:T(8,128)(2,1)S(1)} %get-tuple-element.12.refs_4_), channel_id=1, source_target_pairs={{100,0},{104,4},{108,8},{112,12},{116,16},{120,20},{124,24},{132,3... | collective-permute-start | bytes 393224 | tf_op jit(solution)/shard_map/ppermute | solution.py:37
  43.2 22.8 %collective-permute-start.4 = (bf16[128,512]{1,0:T(8,128)(2,1)S(1)}, bf16[128,512]{1,0:T(8,128)(2,1)S(1)}, u32[]{:S(2)}, u32[]{:S(2)}) collective-permute-start(bf16[128,512]{1,0:T(8,128)(2,1)S(1)} %get-tuple-element.13.refs_5_), channel_id=1, source_target_pairs={{68,0},{72,4},{76,8},{80,12},{84,16},{88,20},{92,24},{100,32},{104... | collective-permute-start | bytes 393224 | tf_op jit(solution)/shard_map/ppermute | solution.py:37
  44.6 21.5 %collective-permute-start.5 = (bf16[128,512]{1,0:T(8,128)(2,1)S(1)}, bf16[128,512]{1,0:T(8,128)(2,1)S(1)}, u32[]{:S(2)}, u32[]{:S(2)}) collective-permute-start(bf16[128,512]{1,0:T(8,128)(2,1)S(1)} %get-tuple-element.14.refs_6_), channel_id=1, source_target_pairs={{36,0},{40,4},{44,8},{48,12},{52,16},{56,20},{60,24},{68,32},{72,3... | collective-permute-start | bytes 393224 | tf_op jit(solution)/shard_map/ppermute | solution.py:37
  45.9 20.2 %collective-permute-start.6 = (bf16[128,512]{1,0:T(8,128)(2,1)S(1)}, bf16[128,512]{1,0:T(8,128)(2,1)S(1)}, u32[]{:S(2)}, u32[]{:S(2)}) collective-permute-start(bf16[128,512]{1,0:T(8,128)(2,1)S(1)} %get-tuple-element.15.refs_7_), channel_id=1, source_target_pairs={{4,0},{8,4},{12,8},{16,12},{20,16},{24,20},{28,24},{5,1},{9,5},{13... | collective-permute-start | bytes 393224 | tf_op jit(solution)/shard_map/ppermute | solution.py:37
  49.1 21.7 %collective-permute-start.10 = (bf16[64,512]{1,0:T(8,128)(2,1)S(1)}, bf16[64,512]{1,0:T(8,128)(2,1)S(1)}, u32[]{:S(2)}, u32[]{:S(2)}) collective-permute-start(bf16[64,512]{1,0:T(8,128)(2,1)S(1)} %slice.16), channel_id=1, source_target_pairs={{0,128},{32,160},{64,192},{96,224},{128,256},{160,288},{192,320},{... | collective-permute-start | bytes 196616 | tf_op jit(solution)/shard_map/ppermute | solution.py:37
  59.7 13.7 %collective-permute-start.11 = (bf16[64,512]{1,0:T(8,128)(2,1)S(1)}, bf16[64,512]{1,0:T(8,128)(2,1)S(1)}, u32[]{:S(2)}, u32[]{:S(2)}) collective-permute-start(bf16[64,512]{1,0:T(8,128)(2,1)S(1)} %slice.17), channel_id=1, source_target_pairs={{0,384},{32,416},{64,448},{96,480},{128,0},{160,32},{192,64},{224,... | collective-permute-start | bytes 196616 | tf_op jit(solution)/shard_map/ppermute | solution.py:37
  66.9 14.4 %all-to-all-start = ((bf16[4,144,512]{2,1,0:T(8,128)(2,1)}), bf16[4,144,512]{2,1,0:T(8,128)(2,1)S(1)}, u32[]{:S(2)}, u32[]{:S(2)}) async-start(bf16[4,144,512]{2,1,0:T(8,128)(2,1)} %shard_map.134), calls=%async_computation | async-start | bytes 1179648 | tf_op jit(solution)/shard_map/all_to_all | solution.py:365
  73.4 18.0 %collective-permute-start.14 = (bf16[512,512]{1,0:T(8,128)(2,1)S(1)}, bf16[512,512]{1,0:T(8,128)(2,1)S(1)}, u32[]{:S(2)}, u32[]{:S(2)}) collective-permute-start(bf16[512,512]{1,0:T(8,128)(2,1)S(1)} %shard_map.135.refs_0_), channel_id=1, source_target_pairs={{0,480},{32,0},{64,32},{96,64},{128,96},{160,128},{192,160},{224,1... | collective-permute-start | bytes 1572872 | tf_op jit(solution)/shard_map/ppermute | solution.py:37
  75.4 18.8 %collective-permute-start.12 = (bf16[512,512]{1,0:T(8,128)(2,1)S(1)}, bf16[512,512]{1,0:T(8,128)(2,1)S(1)}, u32[]{:S(2)}, u32[]{:S(2)}) collective-permute-start(bf16[512,512]{1,0:T(8,128)(2,1)S(1)} %shard_map.135.refs_0_), channel_id=1, source_target_pairs={{0,32},{32,64},{64,96},{96,128},{128,160},{160,192},{192,224},{224... | collective-permute-start | bytes 1572872 | tf_op jit(solution)/shard_map/ppermute | solution.py:37
  82.0 22.0 %all-to-all-start.3 = ((f32[16,1,512]{2,1,0:T(1,128)}), f32[16,1,512]{2,1,0:T(1,128)S(1)}, u32[]{:S(2)}, u32[]{:S(2)}) async-start(f32[16,1,512]{2,1,0:T(1,128)} %copy.19), calls=%async_computation.3 | async-start | bytes 65536 | tf_op jit(solution)/shard_map/all_to_all | solution.py:368
  103.9 23.2 %all-to-all-start.2 = ((bf16[4,12,128,128]{3,2,1,0:T(8,128)(2,1)}), bf16[4,12,128,128]{3,2,1,0:T(8,128)(2,1)S(1)}, u32[]{:S(2)}, u32[]{:S(2)}) async-start(bf16[4,12,128,128]{3,2,1,0:T(8,128)(2,1)} %shard_map.137), calls=%async_computation.2 | async-start | bytes 3145728 | tf_op jit(solution)/shard_map/all_to_all | solution.py:372
  108.2 22.3 %copy-start.5 = (s32[12]{0:T(128)S(1)}, s32[12]{0:T(128)}, u32[]{:S(2)}) copy-start(s32[12]{0:T(128)} %constant.50.clone) | copy-start | bytes 148
  108.2 22.4 %copy-start.4 = (s32[4]{0:T(128)S(1)}, s32[4]{0:T(128)}, u32[]{:S(2)}) copy-start(s32[4]{0:T(128)} %constant.51.clone) | copy-start | bytes 52
  108.2 8.3 %collective-permute-start.15 = (bf16[256,512]{1,0:T(8,128)(2,1)S(1)}, bf16[256,512]{1,0:T(8,128)(2,1)S(1)}, u32[]{:S(2)}, u32[]{:S(2)}) collective-permute-start(bf16[256,512]{1,0:T(8,128)(2,1)S(1)} %slice.21), channel_id=1, source_target_pairs={{0,480},{32,0},{64,32},{96,64},{128,96},{160,128},{192,160},{224,1... | collective-permute-start | bytes 786440 | tf_op jit(solution)/shard_map/ppermute | solution.py:37
  111.2 9.5 %collective-permute-start.13 = (bf16[256,512]{1,0:T(8,128)(2,1)S(1)}, bf16[256,512]{1,0:T(8,128)(2,1)S(1)}, u32[]{:S(2)}, u32[]{:S(2)}) collective-permute-start(bf16[256,512]{1,0:T(8,128)(2,1)S(1)} %slice.20), channel_id=1, source_target_pairs={{0,32},{32,64},{64,96},{96,128},{128,160},{160,192},{192,224},{224... | collective-permute-start | bytes 786440 | tf_op jit(solution)/shard_map/ppermute | solution.py:37
  127.1 11.5 %all-to-all-start.1 = ((bf16[4,4,128,128]{3,2,1,0:T(8,128)(2,1)}), bf16[4,4,128,128]{3,2,1,0:T(8,128)(2,1)S(1)}, u32[]{:S(2)}, u32[]{:S(2)}) async-start(bf16[4,4,128,128]{3,2,1,0:T(8,128)(2,1)} %shard_map.136), calls=%async_computation.1 | async-start | bytes 1048576 | tf_op jit(solution)/shard_map/all_to_all | solution.py:372
  (2 other events, 2.1 us)
